TPU v7x, 256 devices: a whole 4x4x8 slice. The times are simulated.
256 devices in a mesh: grp: 4 (over y), dev: 64 (over z, x, core).
Axes of the slice: x: 4, y: 4, z: 8, core: 2. Of those that a mesh axis runs over, the one named last changes fastest.
Arguments:
- songs: bfloat16 [1024, 48, 768], P(('grp', 'dev')), may hold values from -4 to 4
- gain: float32 [768], replicated, may hold values from 0.5 to 1.5
- enc_weight: bfloat16 [768, 768], replicated, may hold values from -0.21875 to 0.21875
- score_vec: float32 [768], replicated, may hold values from -4 to 4
- left_local: int32 [32768], P(('grp', 'dev')), may hold values from 0 to 3
- right_song: int32 [32768], P(('grp', 'dev')), may hold values from 0 to 1023, as said below
- clique: int32 [1024], replicated, may hold values from 0 to 2
Outputs:
- grad_feats: float32 [1024, 48, 768], P(('grp', 'dev'))
- grad_weight: float32 [768, 768], replicated
- grad_score: float32 [768], replicated
Inputs may be any that keep to these rules, and one draw needn't show every extreme that they name: right_song[p] names a song held by a device whose grp index equals that of the device holding pair p; among the pairs held by one device, the songs held by any one device appear as at most one distinct song.
All inputs are finite; a program needn't handle non-finite values.
Results may differ from a plain program's by a relative error of at most 0.012.
The roundings to bfloat16 on the way count: a program that leaves them out, or rounds other values in their place, can miss the bound.
Values may be sent and summed in bfloat16 or wider, within the bound.
A program may use at most 128 MiB of HBM per device.

v0:
```python
import math

import jax
import jax.numpy as jnp
from jax import lax
from jax.sharding import PartitionSpec as P

loss_scale = 16.0


def encode(songs, gain, enc_weight):
    values = songs.astype(jnp.float32)
    square_mean = jnp.mean(values * values, axis=-1, keepdims=True)
    hidden = (values * lax.rsqrt(square_mean + 1e-06) * gain).astype(jnp.bfloat16)
    model_width = values.shape[-1]
    projected = jnp.dot(
        hidden.reshape(-1, model_width), enc_weight, preferred_element_type=jnp.float32
    )
    features = (values + projected.reshape(values.shape)).astype(jnp.bfloat16)
    return (hidden, features)


def pair_loss(left_values, right_values, score_vec, sign_label):
    left_half = left_values.astype(jnp.bfloat16)
    right_half = right_values.astype(jnp.bfloat16)
    frames = left_half.shape[0]
    model_width = left_half.shape[1]
    scores = jnp.dot(left_half, right_half.T, preferred_element_type=jnp.float32) / math.sqrt(
        model_width
    )
    attn_left = jax.nn.softmax(scores, axis=-1).astype(jnp.bfloat16)
    attn_right = jax.nn.softmax(scores.T, axis=-1).astype(jnp.bfloat16)
    out_left = jnp.dot(attn_left, right_half, preferred_element_type=jnp.float32)
    out_right = jnp.dot(attn_right, left_half, preferred_element_type=jnp.float32)
    pooled = (
        jnp.sum(out_left * left_half.astype(jnp.float32), axis=0)
        + jnp.sum(out_right * right_half.astype(jnp.float32), axis=0)
    ) / math.sqrt(frames)
    logit_value = jnp.sum(pooled * score_vec) / math.sqrt(model_width)
    return loss_scale * jax.nn.softplus(-sign_label * logit_value)


def pair_grads(left_frames, right_frames, score_vec, sign_label):

    def term(left_values, right_values, score_values):
        return pair_loss(left_values, right_values, score_values, sign_label)

    loss_value, pullback = jax.vjp(
        term, left_frames.astype(jnp.float32), right_frames.astype(jnp.float32), score_vec
    )
    return pullback(jnp.ones_like(loss_value))


def local(songs, gain, enc_weight, score_vec, left_local, right_song, clique):
    song_count, frames, model_width = songs.shape
    pair_count = left_local.shape[0]
    peer_count = lax.axis_size("dev")
    group_index = lax.axis_index("grp")
    peer_index = lax.axis_index("dev")
    group_first = group_index * peer_count * song_count
    own_first = (group_index * peer_count + peer_index) * song_count
    hidden, features = encode(songs, gain, enc_weight)
    relative = right_song - group_first
    owner_slot = relative // song_count
    position = relative % song_count
    peer_ids = jnp.arange(peer_count, dtype=jnp.int32)
    owner_match = owner_slot[:, None] == peer_ids[None, :]
    wanted = jnp.max(jnp.where(owner_match, position[:, None], -1), axis=0)
    asked_for = lax.all_to_all(
        wanted.reshape(peer_count, 1), "dev", split_axis=0, concat_axis=0, tiled=True
    )
    asked_index = jnp.maximum(asked_for.reshape(peer_count), 0)
    source = lax.all_gather(features, "dev", axis=0, tiled=True)
    signs = jnp.where(
        jnp.take(clique, own_first + left_local) == jnp.take(clique, right_song), 1.0, -1.0
    ).astype(jnp.float32)
    block_size = min(16, pair_count)
    block_count = pair_count // block_size
    batched = jax.vmap(pair_grads, in_axes=(0, 0, None, 0))

    def accumulate(totals, block_items):
        own_sum, slot_sum, score_sum = totals
        left_index, right_index, sign_block, slot_block = block_items
        left_frames = jnp.take(features, left_index, axis=0)
        right_frames = jnp.take(source, right_index, axis=0)
        grad_left, grad_right, grad_score = batched(
            left_frames, right_frames, score_vec, sign_block
        )
        own_sum = own_sum.at[left_index].add(grad_left)
        slot_sum = slot_sum.at[slot_block].add(grad_right)
        return ((own_sum, slot_sum, score_sum + jnp.sum(grad_score, axis=0)), None)

    block_items = (
        left_local.reshape(block_count, block_size),
        relative.reshape(block_count, block_size),
        signs.reshape(block_count, block_size),
        owner_slot.reshape(block_count, block_size),
    )
    start_totals = (
        jnp.zeros((song_count, frames, model_width), jnp.float32),
        jnp.zeros((peer_count, frames, model_width), jnp.float32),
        jnp.zeros((model_width,), jnp.float32),
    )
    (own_sum, slot_sum, score_sum), _ = lax.scan(accumulate, start_totals, block_items)
    returned = lax.all_to_all(
        slot_sum.astype(jnp.bfloat16), "dev", split_axis=0, concat_axis=0, tiled=True
    ).astype(slot_sum.dtype)
    grad_feats = own_sum.at[asked_index].add(returned)
    local_weight = jnp.dot(
        hidden.reshape(-1, model_width).astype(jnp.float32).T,
        grad_feats.reshape(-1, model_width),
        precision=lax.Precision.HIGHEST,
    )
    grad_weight, grad_score = lax.psum((local_weight, score_sum), ("grp", "dev"))
    return (grad_feats, grad_weight, grad_score)


def solution(mesh):
    in_specs = (
        P(("grp", "dev"), None, None),
        P(),
        P(),
        P(),
        P(("grp", "dev")),
        P(("grp", "dev")),
        P(),
    )
    out_specs = (P(("grp", "dev"), None, None), P(), P())
    return jax.shard_map(local, mesh=mesh, in_specs=in_specs, out_specs=out_specs, check_vma=False)
```

profile of v0, /device:TPU:1, one launch (start us, length us, event | category | flops | bytes accessed | tf_op | source)
XLA Modules:
  0.0 852.7 jit_solution(14437642557082686654)
XLA Ops:
  12.1 13.2 %all-to-all-start = ((s32[64,1,1]{2,1,0:T(1,128)}), s32[64,1,1]{2,1,0:T(1,128)}, u32[]{:S(2)}, u32[]{:S(2)}) async-start(s32[64,1,1]{2,1,0:T(1,128)} %copy.32), calls=%async_computation | async-start | bytes 65536 | tf_op jit(solution)/shard_map/all_to_all | solution.py:69
  28.3 92.3 %all-gather.2.cloned.1.call-done = bf16[256,48,768]{2,1,0:T(8,128)(2,1)} async-done(((bf16[4,48,768]{2,1,0:T(8,128)(2,1)}), bf16[256,48,768]{2,1,0:T(8,128)(2,1)}) %all-gather.2.cloned.1.call-update) | async-done | bytes 18874384 | tf_op jit(solution)/shard_map/all_gather | solution.py:73
  120.6 4.9 broadcast_in_dim.99
  125.5 317.4 %while.17 = (s32[]{:T(128)}, f32[4,48,768]{2,1,0:T(8,128)S(1)}, f32[64,48,768]{2,1,0:T(8,128)}, f32[768]{0:T(1024)S(1)}, s32[8,16]{1,0:T(8,128)S(1)}, /*index=5*...) while((s32[]{:T(128)}, f32[4,48,768]{2,1,0:T(8,128)S(1)}, ...), condition=%wide.region_14.16_spmd.clone, body=%wide.region_1.15_spmd.clone.sunk | while | flops 537656576 | bytes 78630568 | solution.py:104
  127.4 7.0 gather_fusion
  147.0 5.5 fusion.83
  167.0 7.0 gather_fusion
  186.6 5.5 fusion.83
  199.9 4.8 scatter_fusion.1
  206.6 7.0 gather_fusion
  226.2 5.5 fusion.83
  239.6 4.8 scatter_fusion.1
  246.3 7.0 gather_fusion
  265.9 5.5 fusion.83
  279.2 4.8 scatter_fusion.1
  286.0 7.0 gather_fusion
  305.6 5.5 fusion.83
  325.6 7.0 gather_fusion
  345.1 5.5 fusion.83
  358.5 4.9 scatter_fusion.1
  365.3 7.0 gather_fusion
  384.9 5.5 fusion.83
  404.9 7.0 gather_fusion
  424.5 5.5 fusion.83
  437.8 4.9 scatter_fusion.1
  442.9 6.4 convert_element_type.130
  449.3 6.4 all-to-all-start.1
  457.8 103.2 %all-to-all-done.1 = bf16[64,48,768]{2,1,0:T(8,128)(2,1)} async-done(((bf16[64,48,768]{2,1,0:T(8,128)(2,1)}), bf16[64,48,768]{2,1,0:T(8,128)(2,1)}, u32[]{:S(2)}, u32[]{:S(2)}) %all-to-all-start.1) | async-done | bytes 4718624 | tf_op jit(solution)/shard_map/all_to_all | solution.py:105
  561.0 7.2 convert_element_type.131
  568.2 13.2 %scatter_fusion.2 = f32[4,48,768]{2,1,0:T(8,128)S(1)} fusion(f32[4,48,768]{2,1,0:T(8,128)S(1)} %get-tuple-element.401, s32[64]{0:T(128)S(1)} %maximum_reduce_fusion, f32[64,48,768]{2,1,0:T(8,128)} %convert_element_type.131), kind=kCustom, calls=%fused_computation.6 | custom fusion | flops 2359296 | bytes 28311808 | tf_op jit(solution)/shard_map/scatter-add | solution.py:108
  584.1 77.9 %psum.15 = f32[768]{0:T(1024)} all-reduce(f32[768]{0:T(1024)S(1)} %get-tuple-element.403), channel_id=1, replica_groups=mesh['grp'=4,'dev'=64] {'grp','dev'}, use_global_device_ids=true, to_apply=%region_18.20 | all-reduce | flops 768 | bytes 6144 | tf_op jit(solution)/shard_map/psum | solution.py:114
  662.0 180.5 %all-reduce.2.cloned.1.call-done = f32[768,768]{1,0:T(8,128)} async-done(((f32[768,768]{1,0:T(8,128)}), f32[768,768]{1,0:T(8,128)}) %all-reduce.2.cloned.1.call-update) | async-done | bytes 2359312 | tf_op jit(solution)/shard_map/psum | solution.py:114
  (702 shorter events, 205.7 us)
Async XLA Ops:
  7.2 113.4 %all-gather.2.cloned.1.call-start = ((), (), s32[]{:S(2)}) async-start(), calls=%async_computation.2 | async-start | bytes 19169280 | tf_op jit(solution)/shard_map/all_gather | solution.py:73
  9.0 16.5 %copy-start.35 = (s32[128]{0:T(128)S(1)}, s32[128]{0:T(128)}, u32[]{:S(2)}) copy-start(s32[128]{0:T(128)} %param.15) | copy-start | bytes 1540
  9.0 16.6 %copy-start.3 = (s32[1024]{0:T(1024)S(1)}, s32[1024]{0:T(1024)}, u32[]{:S(2)}) copy-start(s32[1024]{0:T(1024)} %param.17) | copy-start | bytes 12292
  12.1 437.2 %all-to-all-start = ((s32[64,1,1]{2,1,0:T(1,128)}), s32[64,1,1]{2,1,0:T(1,128)}, u32[]{:S(2)}, u32[]{:S(2)}) async-start(s32[64,1,1]{2,1,0:T(1,128)} %copy.32), calls=%async_computation | async-start | bytes 65536 | tf_op jit(solution)/shard_map/all_to_all | solution.py:69
  126.7 12.4 %copy-start.21 = (pred[16]{0:T(512)(128)(4,1)}, pred[16]{0:T(512)(128)(4,1)S(1)}, u32[]{:S(2)}) copy-start(pred[16]{0:T(512)(128)(4,1)S(1)} %get-tuple-element.317) | copy-start | bytes 52 | tf_op jit(solution)/shard_map/while
  126.7 12.4 %copy-start.23 = (pred[16]{0:T(512)(128)(4,1)}, pred[16]{0:T(512)(128)(4,1)S(1)}, u32[]{:S(2)}) copy-start(pred[16]{0:T(512)(128)(4,1)S(1)} %get-tuple-element.316) | copy-start | bytes 52 | tf_op jit(solution)/shard_map/while
  134.9 7.9 copy-start.11
  166.3 12.4 %copy-start.21 = (pred[16]{0:T(512)(128)(4,1)}, pred[16]{0:T(512)(128)(4,1)S(1)}, u32[]{:S(2)}) copy-start(pred[16]{0:T(512)(128)(4,1)S(1)} %get-tuple-element.317) | copy-start | bytes 52 | tf_op jit(solution)/shard_map/while
  166.3 12.4 %copy-start.23 = (pred[16]{0:T(512)(128)(4,1)}, pred[16]{0:T(512)(128)(4,1)S(1)}, u32[]{:S(2)}) copy-start(pred[16]{0:T(512)(128)(4,1)S(1)} %get-tuple-element.316) | copy-start | bytes 52 | tf_op jit(solution)/shard_map/while
  174.6 7.9 copy-start.11
  205.9 12.4 %copy-start.21 = (pred[16]{0:T(512)(128)(4,1)}, pred[16]{0:T(512)(128)(4,1)S(1)}, u32[]{:S(2)}) copy-start(pred[16]{0:T(512)(128)(4,1)S(1)} %get-tuple-element.317) | copy-start | bytes 52 | tf_op jit(solution)/shard_map/while
  205.9 12.4 %copy-start.23 = (pred[16]{0:T(512)(128)(4,1)}, pred[16]{0:T(512)(128)(4,1)S(1)}, u32[]{:S(2)}) copy-start(pred[16]{0:T(512)(128)(4,1)S(1)} %get-tuple-element.316) | copy-start | bytes 52 | tf_op jit(solution)/shard_map/while
  214.2 7.9 copy-start.11
  245.6 12.4 %copy-start.21 = (pred[16]{0:T(512)(128)(4,1)}, pred[16]{0:T(512)(128)(4,1)S(1)}, u32[]{:S(2)}) copy-start(pred[16]{0:T(512)(128)(4,1)S(1)} %get-tuple-element.317) | copy-start | bytes 52 | tf_op jit(solution)/shard_map/while
  245.6 12.4 %copy-start.23 = (pred[16]{0:T(512)(128)(4,1)}, pred[16]{0:T(512)(128)(4,1)S(1)}, u32[]{:S(2)}) copy-start(pred[16]{0:T(512)(128)(4,1)S(1)} %get-tuple-element.316) | copy-start | bytes 52 | tf_op jit(solution)/shard_map/while
  253.9 7.9 copy-start.11
  285.3 12.4 %copy-start.21 = (pred[16]{0:T(512)(128)(4,1)}, pred[16]{0:T(512)(128)(4,1)S(1)}, u32[]{:S(2)}) copy-start(pred[16]{0:T(512)(128)(4,1)S(1)} %get-tuple-element.317) | copy-start | bytes 52 | tf_op jit(solution)/shard_map/while
  285.3 12.4 %copy-start.23 = (pred[16]{0:T(512)(128)(4,1)}, pred[16]{0:T(512)(128)(4,1)S(1)}, u32[]{:S(2)}) copy-start(pred[16]{0:T(512)(128)(4,1)S(1)} %get-tuple-element.316) | copy-start | bytes 52 | tf_op jit(solution)/shard_map/while
  293.5 7.9 copy-start.11
  324.8 12.4 %copy-start.21 = (pred[16]{0:T(512)(128)(4,1)}, pred[16]{0:T(512)(128)(4,1)S(1)}, u32[]{:S(2)}) copy-start(pred[16]{0:T(512)(128)(4,1)S(1)} %get-tuple-element.317) | copy-start | bytes 52 | tf_op jit(solution)/shard_map/while
  324.8 12.4 %copy-start.23 = (pred[16]{0:T(512)(128)(4,1)}, pred[16]{0:T(512)(128)(4,1)S(1)}, u32[]{:S(2)}) copy-start(pred[16]{0:T(512)(128)(4,1)S(1)} %get-tuple-element.316) | copy-start | bytes 52 | tf_op jit(solution)/shard_map/while
  333.1 7.9 copy-start.11
  364.6 12.4 %copy-start.21 = (pred[16]{0:T(512)(128)(4,1)}, pred[16]{0:T(512)(128)(4,1)S(1)}, u32[]{:S(2)}) copy-start(pred[16]{0:T(512)(128)(4,1)S(1)} %get-tuple-element.317) | copy-start | bytes 52 | tf_op jit(solution)/shard_map/while
  364.6 12.4 %copy-start.23 = (pred[16]{0:T(512)(128)(4,1)}, pred[16]{0:T(512)(128)(4,1)S(1)}, u32[]{:S(2)}) copy-start(pred[16]{0:T(512)(128)(4,1)S(1)} %get-tuple-element.316) | copy-start | bytes 52 | tf_op jit(solution)/shard_map/while
  372.8 7.9 copy-start.11
  404.2 12.4 %copy-start.21 = (pred[16]{0:T(512)(128)(4,1)}, pred[16]{0:T(512)(128)(4,1)S(1)}, u32[]{:S(2)}) copy-start(pred[16]{0:T(512)(128)(4,1)S(1)} %get-tuple-element.317) | copy-start | bytes 52 | tf_op jit(solution)/shard_map/while
  404.2 12.4 %copy-start.23 = (pred[16]{0:T(512)(128)(4,1)}, pred[16]{0:T(512)(128)(4,1)S(1)}, u32[]{:S(2)}) copy-start(pred[16]{0:T(512)(128)(4,1)S(1)} %get-tuple-element.316) | copy-start | bytes 52 | tf_op jit(solution)/shard_map/while
  449.3 111.6 %all-to-all-start.1 = ((bf16[64,48,768]{2,1,0:T(8,128)(2,1)}), bf16[64,48,768]{2,1,0:T(8,128)(2,1)}, u32[]{:S(2)}, u32[]{:S(2)}) async-start(bf16[64,48,768]{2,1,0:T(8,128)(2,1)} %convert_element_type.130), calls=%async_computation.1 | async-start | bytes 9437184 | tf_op jit(solution)/shard_map/all_to_all | solution.py:105
  455.7 386.8 %all-reduce.2.cloned.1.call-start = ((), (), s32[]{:S(2)}) async-start(), calls=%async_computation.3 | async-start | bytes 4718592 | tf_op jit(solution)/shard_map/psum | solution.py:114
  568.2 13.2 %copy-start.16 = (bf16[4,48,768]{2,1,0:T(8,128)(2,1)S(1)}, bf16[4,48,768]{2,1,0:T(8,128)(2,1)}, u32[]{:S(2)}) copy-start(bf16[4,48,768]{2,1,0:T(8,128)(2,1)} %param.11) | copy-start | bytes 884740
  568.2 13.2 %copy-start.34 = (f32[4,48]{1,0:T(4,128)S(1)}, f32[4,48]{1,0:T(4,128)}, u32[]{:S(2)}) copy-start(f32[4,48]{1,0:T(4,128)} %copy-done.33) | copy-start | bytes 2308
  568.2 13.2 %copy-start.37 = (f32[768]{0:T(1024)S(1)}, f32[768]{0:T(1024)}, u32[]{:S(2)}) copy-start(f32[768]{0:T(1024)} %param.12) | copy-start | bytes 9220
  (192 other events, 486.4 us)
Sparse Core Ops, SparseCore 0:
  11.4 109.1 all-gather.1
  584.2 258.2 all-reduce.1
where the time goes:
time: 856 us; the launch traced here: 853 us
  waiting for transfers between devices  376 us (44%)
  matrix products  152 us (18%)
  other arithmetic  123 us (14%)
  local copies, waits for them, and re-layouts  85.9 us (10%)
  blocking collectives  77.9 us (9%)
  starting transfers between devices  19.6 us (2%)
  between operations  14.2 us (2%)
    psum x1, waiting for transfers between devices, local(): lax.psum((local_weight, score_sum), ('grp', 'dev'))  181 us
    all_to_all x1, waiting for transfers between devices, local(): lax.all_to_all(slot_sum.astype(jnp.bfloat16), 'dev', split_axis=0, concat...  103 us
    all_gather x1, waiting for transfers between devices, local(): source = lax.all_gather(features, 'dev', axis=0, tiled=True)  92.3 us
    psum x1, blocking collectives, local(): lax.psum((local_weight, score_sum), ('grp', 'dev'))  77.9 us
    dot_general x24, matrix products, pair_loss(): jnp.dot(attn_left, right_half, preferred_element_type=jnp.float32)  73.8 us
    gather x8, local copies, waits for them, and re-layouts, accumulate(): right_frames = jnp.take(source, right_index, axis=0)  55.9 us
    dot_general x24, matrix products, pair_loss(): jnp.dot(attn_right, left_half, preferred_element_type=jnp.float32)  46 us
    scatter-add x8, other arithmetic, accumulate(): slot_sum = slot_sum.at[slot_block].add(grad_right)  38.5 us
  transfers between devices with their start and end apart: 4, of which 3 were waited for; matrix products, arithmetic and copies ran while one was open for 37% of the time, Pallas kernels for 0%

commit v1 on v0

v1 whole, which is shorter than its diff:
```python
import functools
import math

import jax
import jax.numpy as jnp
from jax import lax
from jax.experimental import pallas as pl
from jax.experimental.pallas import tpu as pltpu
from jax.sharding import PartitionSpec as P

D = 768
FR = 48
OWN = 4 * FR
UNIT = 2 * FR
BLK = D // 128
UROWS = UNIT * BLK + 16
LANES = 8 * FR
RING = 32
NB = 32
LOSS_SCALE = 16.0
LOG2E = math.log2(math.e)
C0 = 1.0 / (math.sqrt(FR) * math.sqrt(D))
F32 = jnp.float32
BF16 = jnp.bfloat16
MESH = pl.DeviceIdType.MESH


def ring_pos(z, x):
    u = (z - 3 * x + 24) % 8
    return (4 * z + (x + z) % 4, 4 * x + 16 * (u // 4) + u % 4)


def ring_chip(k, i):
    if k == 0:
        z = i // 4
        return z * 4 + (i % 4 - z + 8) % 4
    j = i // 4
    return ((3 * j + i % 4) % 8) * 4 + j % 4


def dot_nn(a, b):
    return jnp.dot(a, b, preferred_element_type=F32)


def dot_nt(a, b):
    return lax.dot_general(a, b, (((1,), (1,)), ((), ())), preferred_element_type=F32)


def dot_tn(a, b):
    return lax.dot_general(a, b, (((0,), (0,)), ((), ())), preferred_element_type=F32)


def col_softmax(scores):
    scale = LOG2E / math.sqrt(D)
    top = jnp.max(scores, axis=0, keepdims=True)
    e = jnp.exp2((scores - top) * scale)
    return e * (1.0 / jnp.sum(e, axis=0, keepdims=True))


def batch_terms(peer, own_t, own_st, seg, weights, signs):
    scores_x = dot_nn(peer, own_t)
    by_peer = jnp.concatenate(
        [col_softmax(scores_x[p * FR : (p + 1) * FR]) for p in range(8)], axis=0
    )
    by_peer = by_peer.T[:OWN].astype(BF16)
    both = dot_nt(own_st, peer)
    total, first, second, z1s = [], [], [], []
    for a in range(4):
        rows = slice(a * FR, (a + 1) * FR)
        t = both[OWN + a * FR : OWN + (a + 1) * FR]
        p1 = by_peer[rows].astype(F32)
        p2 = col_softmax(both[rows]).astype(BF16).astype(F32)
        z1 = p1 * t
        z2 = p2 * t
        r2 = jnp.sum(z2, axis=0, keepdims=True)
        total.append(jnp.sum(z1, axis=0, keepdims=True) + r2)
        z1s.append(z1.astype(BF16))
        first.append(p1 + p2)
        second.append((z1 + z2 - p2 * r2, p1))
    sums = jnp.concatenate(total + [jnp.zeros((4, LANES), F32)], axis=0)
    high = sums.astype(BF16)
    low = (sums - high.astype(F32)).astype(BF16)
    spread = dot_nn(jnp.concatenate([high, low], axis=0), seg)
    logit = (spread[:8] + spread[8:]) * C0
    coef = weights * signs * (-LOSS_SCALE * C0) / (1.0 + jnp.exp(signs * logit))
    r1 = dot_nn(jnp.concatenate(z1s, axis=0), seg)
    out1, out2 = [], []
    for a in range(4):
        c = coef[a : a + 1]
        g, p1 = second[a]
        out1.append((c * first[a]).astype(BF16))
        out2.append((c * (g - p1 * r1[a * FR : (a + 1) * FR])).astype(BF16))
    return jnp.concatenate(out1 + out2, axis=0)


def pair_kernel(
    x_ref, gain_ref, w_ref, v_ref, meta_ref, ws_ref,
    gf_ref, hid_ref, gs_ref,
    buf, own_st, own_t, seg, ind8, ind_m, sel, acc, ssem, rsem,
):
    grp = lax.axis_index("grp")
    me = lax.axis_index("dev")
    core = me % 2
    chip = me // 2
    sib = me + 1 - 2 * core
    pos = ring_pos(chip // 4, chip % 4)
    near = [
        [ring_chip(k, (pos[k] + step) % RING) * 2 + core for k in range(2)]
        for step in (1, RING - 1)
    ]

    barrier = pltpu.get_barrier_semaphore()
    for dev in near[0] + near[1] + [sib]:
        pl.semaphore_signal(barrier, inc=1, device_id=(grp, dev), device_id_type=MESH)

    def remote(sb, su, db, du, dev):
        return pltpu.make_async_remote_copy(
            src_ref=buf.at[sb, su],
            dst_ref=buf.at[db, du],
            send_sem=ssem.at[db, du],
            recv_sem=rsem.at[db, du],
            device_id=(grp, dev),
            device_id_type=MESH,
        )

    def arrived(b, u):
        remote(b, u, b, u, sib).wait_recv()

    values = x_ref[...].astype(F32)
    square_mean = jnp.mean(values * values, axis=-1, keepdims=True)
    hidden = (values * lax.rsqrt(square_mean + 1e-06) * gain_ref[...]).astype(BF16)
    hid_ref[...] = hidden
    feats = (values + dot_nn(hidden, w_ref[...])).astype(BF16)
    for k in range(2):
        for j in range(BLK):
            buf[0, k, j * UNIT : (j + 1) * UNIT, :] = feats[
                k * UNIT : (k + 1) * UNIT, j * 128 : (j + 1) * 128
            ]
        buf[0, k, BLK * UNIT : UROWS, :] = meta_ref[k]

    pl.semaphore_wait(barrier, 5)
    for k in range(2):
        remote(0, k, 0, 2 + k, sib).start()
        for way in range(2):
            remote(0, k, 1, way * 2 + k, near[way][k]).start()

    own_st[:OWN] = feats
    scaled = (feats.astype(F32) * v_ref[...]).astype(BF16)
    own_st[OWN:] = scaled
    own_t[...] = jnp.concatenate(
        [feats, jnp.zeros((256 - OWN, D), BF16)], axis=0
    ).T

    def ids(shape, dim):
        return lax.broadcasted_iota(jnp.int32, shape, dim)

    def mark(cond):
        return jnp.where(cond, 1.0, 0.0).astype(BF16)

    shape = (LANES, LANES)
    seg[...] = mark(ids(shape, 0) // FR == ids(shape, 1) // FR)
    shape = (128, LANES)
    ind8[...] = mark(ids(shape, 0) == ids(shape, 1) // FR)
    shape = (64, LANES)
    row = ids(shape, 0)
    song = 2 * (row // 16) + (row % 16) // 2
    right_row = jnp.logical_and(row % 16 < 4, row % 2 == me // 32)
    ind_m[...] = mark(jnp.logical_and(right_row, song == ids(shape, 1) // FR))
    shape = (16, 128)
    wanted = jnp.logical_and(ids(shape, 0) < 4, ids(shape, 1) == (me % 32) * 4 + ids(shape, 0))
    sel[...] = mark(wanted)
    acc[...] = jnp.zeros_like(acc)

    def step(b, carry):
        odd = b % 2

        @pl.when(b == 0)
        def _():
            arrived(0, 2)
            arrived(0, 3)

        @pl.when(jnp.logical_and(odd == 1, b < NB - 1))
        def _():
            for u in range(4):
                arrived(b, u)
                if u < 2:
                    remote(b, u, b + 2, u, near[0][u]).start()
                else:

                    @pl.when(b < NB - 3)
                    def _():
                        remote(b, u, b + 2, u, near[1][u - 2]).start()

                remote(b, u, b + 1, u, sib).start()

        @pl.when(jnp.logical_and(odd == 0, b > 0))
        def _():
            for u in range(4):
                arrived(b, u)

        @pl.when(b == NB - 1)
        def _():
            for k in range(2):
                arrived(NB - 1, k)
                remote(NB - 1, k, NB - 1, 2 + k, sib).start()
            for k in range(2):
                arrived(NB - 1, 2 + k)

        peer = jnp.concatenate(
            [
                buf[b, :, j * UNIT : (j + 1) * UNIT, :].reshape(LANES, 128)
                for j in range(BLK)
            ],
            axis=1,
        )
        meta = buf[b, :, BLK * UNIT : UROWS, :].reshape(64, 128)
        wexp = dot_nn(ws_ref[b], ind8[...])
        right = dot_nn(dot_nt(sel[...], meta).astype(BF16), ind_m[...])
        terms = batch_terms(
            peer, own_t[...], own_st[...], seg[...], wexp[:8] + right[:8], wexp[8:]
        )
        acc[...] += dot_nn(terms, peer)
        return carry

    lax.fori_loop(0, NB, step, 0)

    first = acc[:OWN]
    gf_ref[...] = v_ref[...] * first + acc[OWN:] * (1.0 / math.sqrt(D))
    score = 0.5 * jnp.sum(own_st[:OWN].astype(F32) * first, axis=0, keepdims=True)
    gs_ref[...] = jnp.broadcast_to(score, (8, D))

    def drain(b, carry):
        for u in range(4):
            if u < 2:

                @pl.when(b > 0)
                def _():
                    remote(b, u, b, u, sib).wait_send()

            else:
                remote(b, u, b, u, sib).wait_send()
        return carry

    lax.fori_loop(0, NB, drain, 0)


def pair_grads(songs, gain, enc_weight, score_vec, meta, ws):
    vmem = pl.BlockSpec(memory_space=pltpu.VMEM)
    return pl.pallas_call(
        pair_kernel,
        out_shape=(
            jax.ShapeDtypeStruct((OWN, D), F32),
            jax.ShapeDtypeStruct((OWN, D), BF16),
            jax.ShapeDtypeStruct((8, D), F32),
        ),
        in_specs=[vmem] * 6,
        out_specs=(vmem,) * 3,
        scratch_shapes=[
            pltpu.VMEM((NB, 4, UROWS, 128), BF16),
            pltpu.VMEM((2 * OWN, D), BF16),
            pltpu.VMEM((D, 256), BF16),
            pltpu.VMEM((LANES, LANES), BF16),
            pltpu.VMEM((128, LANES), BF16),
            pltpu.VMEM((64, LANES), BF16),
            pltpu.VMEM((16, 128), BF16),
            pltpu.VMEM((2 * OWN, D), F32),
            pltpu.SemaphoreType.DMA((NB, 4)),
            pltpu.SemaphoreType.DMA((NB, 4)),
        ],
        compiler_params=pltpu.CompilerParams(
            collective_id=0, has_side_effects=True, vmem_limit_bytes=52 * 2**20
        ),
    )(songs, gain, enc_weight, score_vec, meta, ws)


FLAT = BLK * D
HALF = FLAT // 2
QUARTER = HALF // 4
PIECE = QUARTER // 4


def reduce_kernel(
    hid_ref, gf_ref, gs_ref,
    out_ref, score_ref,
    flat, rc, sx, rx, sy, ry, rz, full, tc, tx, ty, tz, sems, rems,
):
    y = lax.axis_index("grp")
    me = lax.axis_index("dev")
    core = me % 2
    chip = me // 2
    x = chip % 4
    z = chip // 4
    sib = (y, me + 1 - 2 * core)
    along_x = [(y, (z * 4 + (x + s) % 4) * 2 + core) for s in range(1, 4)]
    along_y = [((y + s) % 4, me) for s in range(1, 4)]
    along_z = [(y, (((z + s) % 8) * 4 + x) * 2 + core) for s in range(1, 8)]

    barrier = pltpu.get_barrier_semaphore()
    for dev in [sib] + along_x + along_y + along_z:
        pl.semaphore_signal(barrier, inc=1, device_id=dev, device_id_type=MESH)

    count = [0]
    pending = []

    def remote(src, dst, dev):
        i = count[0]
        count[0] += 1
        copy = pltpu.make_async_remote_copy(
            src_ref=src, dst_ref=dst, send_sem=sems.at[i], recv_sem=rems.at[i],
            device_id=dev, device_id_type=MESH,
        )
        copy.start()
        pending.append(copy)
        return copy

    def rows(start, size):
        return pl.ds(pl.multiple_of(start, 16), size)

    gf = gf_ref[...]
    high = gf.astype(BF16)
    low = (gf - high.astype(F32)).astype(BF16)
    hidden = hid_ref[...]
    hidden_t = hidden.T
    for j in range(BLK):
        cols = slice(j * 128, (j + 1) * 128)
        part = dot_nn(hidden_t, high[:, cols]) + dot_nn(hidden_t, low[:, cols])
        flat[j * D : (j + 1) * D, :] = part.astype(BF16)
    score = jnp.concatenate(
        [gs_ref[0:1, j * 128 : (j + 1) * 128] for j in range(BLK)]
        + [jnp.zeros((8 - BLK, 128), F32)],
        axis=0,
    )
    pl.semaphore_wait(barrier, 14)

    tc[core] = score
    a = remote(flat.at[rows((1 - core) * HALF, HALF)], rc, sib)
    b = remote(tc.at[core], tc.at[core], sib)
    a.wait_recv()
    b.wait_recv()
    sx[...] = (
        flat[rows(core * HALF, HALF), :].astype(F32) + rc[...].astype(F32)
    ).astype(BF16)
    tx[x] = tc[0] + tc[1]

    copies = []
    for s, dev in enumerate(along_x):
        to = (x + s + 1) % 4
        copies.append(remote(sx.at[rows(to * QUARTER, QUARTER)], rx.at[s], dev))
        copies.append(remote(tx.at[x], tx.at[x], dev))
    for c in copies:
        c.wait_recv()
    sy[...] = (
        sx[rows(x * QUARTER, QUARTER), :].astype(F32)
        + rx[0].astype(F32)
        + rx[1].astype(F32)
        + rx[2].astype(F32)
    ).astype(BF16)
    ty[y] = (tx[0] + tx[1]) + (tx[2] + tx[3])

    copies = []
    for s, dev in enumerate(along_y):
        to = (y + s + 1) % 4
        copies.append(remote(sy.at[rows(to * PIECE, PIECE)], ry.at[s], dev))
        copies.append(remote(ty.at[y], ty.at[y], dev))
    for c in copies:
        c.wait_recv()
    rz[z] = (
        sy[rows(y * PIECE, PIECE), :].astype(F32)
        + ry[0].astype(F32)
        + ry[1].astype(F32)
        + ry[2].astype(F32)
    ).astype(BF16)
    tz[z] = (ty[0] + ty[1]) + (ty[2] + ty[3])

    copies = []
    for dev in along_z:
        copies.append(remote(rz.at[z], rz.at[z], dev))
        copies.append(remote(tz.at[z], tz.at[z], dev))
    for c in copies:
        c.wait_recv()
    total = rz[0].astype(F32)
    score = tz[0]
    for i in range(1, 8):
        total = total + rz[i].astype(F32)
        score = score + tz[i]
    score_ref[...] = score
    first = core * HALF + x * QUARTER
    mine = rows(first + y * PIECE, PIECE)
    full[mine, :] = total.astype(BF16)

    copies = [remote(full.at[mine], full.at[mine], dev) for dev in along_y]
    for c in copies:
        c.wait_recv()
    quarter = rows(first, QUARTER)
    copies = [remote(full.at[quarter], full.at[quarter], dev) for dev in along_x]
    for c in copies:
        c.wait_recv()
    half = rows(core * HALF, HALF)
    remote(full.at[half], full.at[half], sib).wait_recv()
    for j in range(BLK):
        out_ref[:, j * 128 : (j + 1) * 128] = full[j * D : (j + 1) * D, :]
    for c in pending:
        c.wait_send()


def reduce_grads(hidden, grad_feats, score):
    vmem = pl.BlockSpec(memory_space=pltpu.VMEM)
    n_copies = 2 + 6 + 6 + 14 + 3 + 3 + 1
    return pl.pallas_call(
        reduce_kernel,
        out_shape=(
            jax.ShapeDtypeStruct((D, D), BF16),
            jax.ShapeDtypeStruct((8, 128), F32),
        ),
        in_specs=[vmem] * 3,
        out_specs=(vmem,) * 2,
        scratch_shapes=[
            pltpu.VMEM((FLAT, 128), BF16),
            pltpu.VMEM((HALF, 128), BF16),
            pltpu.VMEM((HALF, 128), BF16),
            pltpu.VMEM((3, QUARTER, 128), BF16),
            pltpu.VMEM((QUARTER, 128), BF16),
            pltpu.VMEM((3, PIECE, 128), BF16),
            pltpu.VMEM((8, PIECE, 128), BF16),
            pltpu.VMEM((FLAT, 128), BF16),
            pltpu.VMEM((2, 8, 128), F32),
            pltpu.VMEM((4, 8, 128), F32),
            pltpu.VMEM((4, 8, 128), F32),
            pltpu.VMEM((8, 8, 128), F32),
            pltpu.SemaphoreType.DMA((n_copies,)),
            pltpu.SemaphoreType.DMA((n_copies,)),
        ],
        compiler_params=pltpu.CompilerParams(
            collective_id=1, has_side_effects=True, vmem_limit_bytes=40 * 2**20
        ),
    )(hidden, grad_feats, score)


def batch_songs(me):
    core = me % 2
    chip = me // 2
    pos = ring_pos(chip // 4, chip % 4)
    b = jnp.arange(NB, dtype=jnp.int32)[:, None]
    u = jnp.arange(4, dtype=jnp.int32)[None, :]
    k = u % 2
    ends = jnp.logical_or(b == 0, b == NB - 1)
    t = (b + 1) // 2
    way = jnp.where(jnp.logical_and(u >= 2, jnp.logical_not(ends)), 1, 0)
    at = [(p + jnp.where(way == 1, t, RING - t)) % RING for p in pos]
    origin = jnp.where(k == 0, ring_chip(0, at[0]), ring_chip(1, at[1]))
    other = jnp.where(ends, u // 2, (b + 1) % 2)
    held = origin * 2 + jnp.where(other == 1, 1 - core, core)
    first = held * 4 + 2 * k
    return (first[:, :, None] + jnp.arange(2, dtype=jnp.int32)).reshape(NB, 8)


def pair_tables(left_local, right_rel, clique, group, me):
    hot_left = left_local[None, :] == jnp.arange(4, dtype=jnp.int32)[:, None]
    hot_right = right_rel[:, None] == jnp.arange(256, dtype=jnp.int32)[None, :]
    counts = dot_nn(hot_left.astype(BF16), hot_right.astype(BF16)).astype(BF16)
    meta = counts.reshape(2, 4, 128)
    meta = jnp.pad(meta, ((0, 0), (0, 12), (0, 0)))
    songs = batch_songs(me)
    hot = jnp.arange(256, dtype=jnp.int32)[:, None] == songs.reshape(1, 256)
    own = clique_of(clique, group * 256 + me * 4, 4)
    theirs = clique_of(clique, group * 256, 256)
    signs = jnp.where(own[:, None] == theirs[None, :], 1.0, -1.0).astype(BF16)
    rows = jnp.concatenate([counts, signs], axis=0)
    rows = dot_nn(rows, hot.astype(BF16)).reshape(8, NB, 8)
    rows = rows.transpose(1, 0, 2).astype(BF16)
    ws = jnp.zeros((NB, 16, 128), BF16)
    ws = ws.at[:, 0:4, 0:8].set(rows[:, 0:4]).at[:, 8:12, 0:8].set(rows[:, 4:8])
    return meta, ws


def clique_of(clique, start, size):
    return lax.dynamic_slice_in_dim(clique, start, size)


def local(songs, gain, enc_weight, score_vec, left_local, right_song, clique):
    group = lax.axis_index("grp")
    me = lax.axis_index("dev")
    meta, ws = pair_tables(left_local, right_song - group * 256, clique, group, me)
    gf, hidden, score = pair_grads(
        songs.reshape(OWN, D), gain.reshape(1, D), enc_weight, score_vec.reshape(1, D), meta, ws
    )
    weight, total = reduce_grads(hidden, gf, score)
    return (
        gf.reshape(4, FR, D),
        weight.astype(F32),
        total[:BLK].reshape(D),
    )


def solution(mesh):
    in_specs = (
        P(("grp", "dev"), None, None),
        P(),
        P(),
        P(),
        P(("grp", "dev")),
        P(("grp", "dev")),
        P(),
    )
    out_specs = (P(("grp", "dev"), None, None), P(), P())
    return jax.shard_map(local, mesh=mesh, in_specs=in_specs, out_specs=out_specs, check_vma=False)
```

time: 856 us -> 142 us (0.17)
  waiting for transfers between devices: 376 us -> 0 us
  matrix products: 152 us -> 1.02 us
  Pallas kernels: 0 us -> 131 us
  other arithmetic: 123 us -> 2.58 us
  local copies, waits for them, and re-layouts: 85.9 us -> 5.7 us
  blocking collectives: 77.9 us -> 0 us
  starting transfers between devices: 19.6 us -> 0 us
  between operations: 14.2 us -> 0.85 us
    psum x1 -> x0, waiting for transfers between devices: 181 us -> none  [local(): lax.psum((local_weight, score_sum), ('grp', 'dev'))]
    dot_general x74 -> x2, matrix products: 152 us -> 1.02 us  [dot_nn(): return jnp.dot(a, b, preferred_element_type=F32)]
    pallas_call x0 -> x2, Pallas kernels: none -> 131 us  [the longest x1 91.4 us: pair_grads(): pl.pallas_call(pair_kernel, out_shape=(jax.ShapeDtypeStruct((OWN, D), F32...]
    all_to_all x2 -> x0, waiting for transfers between devices: 103 us -> none  [the longest x1 103 us: local(): lax.all_to_all(slot_sum.astype(jnp.bfloat16), 'dev', split_axis=0, concat...]
    all_gather x1 -> x0, waiting for transfers between devices: 92.3 us -> none  [local(): source = lax.all_gather(features, 'dev', axis=0, tiled=True)]
    scatter-add x17 -> x0, other arithmetic: 82.5 us -> none  [the longest x8 38.5 us: accumulate(): slot_sum = slot_sum.at[slot_block].add(grad_right)]
    psum x1 -> x0, blocking collectives: 77.9 us -> none  [local(): lax.psum((local_weight, score_sum), ('grp', 'dev'))]
    gather x18 -> x0, local copies, waits for them, and re-layouts: 62.8 us -> none  [the longest x8 55.9 us: accumulate(): right_frames = jnp.take(source, right_index, axis=0)]
  transfers between devices with their start and end apart: 4 -> 0, of which waited for: 3 -> 0; matrix products, arithmetic and copies ran while one was open for 37% -> 0% of each run, Pallas kernels for 0% -> 0%
where the time goes in v1:
time: 142 us
  Pallas kernels  131 us (92%)
  local copies, waits for them, and re-layouts  5.7 us (4%)
  other arithmetic  2.58 us (2%)
    pallas_call x1, Pallas kernels, pair_grads(): pl.pallas_call(pair_kernel, out_shape=(jax.ShapeDtypeStruct((OWN, D), F32...  91.4 us
    pallas_call x1, Pallas kernels, reduce_grads(): pl.pallas_call(reduce_kernel, out_shape=(jax.ShapeDtypeStruct((D, D), BF1...  40 us

profile of v1, /device:TPU:1, one launch (start us, length us, event | category | flops | bytes accessed | tf_op | source)
XLA Modules:
  0.0 141.5 jit_solution(17930425259576582109)
XLA Ops:
  0.6 0.0 copy-start
  0.8 0.8 dynamic_slice.6
  1.5 0.7 broadcast_subtract_fusion.1
  2.2 0.8 dynamic_slice.7
  2.9 0.1 select_convert_fusion
  3.1 0.9 convolution_convert_fusion.1
  3.9 0.7 reshape.498.gain_ref
  4.6 0.7 reshape.499.v_ref
  5.3 0.2 fusion.11
  5.5 0.1 iota_add_fusion
  5.6 0.1 add.308
  5.7 0.2 convolution_convert_fusion
  5.9 0.1 convert_element_type.26
  6.1 1.0 scatter.9.ws_ref
  7.1 0.0 copy-done
  7.1 91.4 %shard_map.94 = (f32[192,768]{1,0:T(8,128)S(1)}, bf16[192,768]{1,0:T(8,128)(2,1)S(1)}, f32[8,768]{1,0:T(8,128)S(1)}) custom-call(bf16[192,768]{1,0:T(8,128)(2,1)S(1)} %bitcast.8, f32[1,768]{1,0:T(1,128)S(1)} %reshape.498.gain_ref, bf16[768,768]{1,0:T(8,128)(2,1)} %w_ref.1, f32[1,768]{1,0:T(1,128)S(1)} %reshape.499.v_ref, ...), custom_call_target="tpu_custom_call" | custom-call | tf_op jit(solution)/shard_map/pallas_call | solution.py:249
  98.5 40.0 %shard_map.95 = (bf16[768,768]{1,0:T(8,128)(2,1)S(1)}, f32[8,128]{1,0:T(8,128)S(1)}) custom-call(bf16[192,768]{1,0:T(8,128)(2,1)S(1)} %get-tuple-element.33.hid_ref, f32[192,768]{1,0:T(8,128)S(1)} %get-tuple-element.32.gf_ref, f32[8,768]{1,0:T(8,128)S(1)} %get-tuple-element.34.gs_ref), custom_call_target="tpu_custom_call" | custom-call | tf_op jit(solution)/shard_map/pallas_call | solution.py:409
  138.5 0.6 slice_bitcast_fusion
  139.1 1.6 %convert_element_type.28 = f32[768,768]{1,0:T(8,128)} convert(bf16[768,768]{1,0:T(8,128)(2,1)S(1)} %get-tuple-element.35) | non-fusion elementwise | flops 589824 | bytes 3538944 | tf_op jit(solution)/shard_map/convert_element_type | solution.py:490
  140.7 0.8 copy.15
  (10 shorter events, 0.1 us)
Async XLA Ops:
  0.6 6.5 %copy-start = (bf16[4,48,768]{2,1,0:T(8,128)(2,1)S(1)}, bf16[4,48,768]{2,1,0:T(8,128)(2,1)}, u32[]{:S(2)}) copy-start(bf16[4,48,768]{2,1,0:T(8,128)(2,1)} %param.11) | copy-start | bytes 884740

commit v2 on v1

v2 whole, which is shorter than its diff:
```python
import functools
import math

import jax
import jax.numpy as jnp
from jax import lax
from jax.experimental import pallas as pl
from jax.experimental.pallas import tpu as pltpu
from jax.sharding import PartitionSpec as P

D = 768
FR = 48
OWN = 4 * FR
OWN2 = 2 * OWN
UNIT = 2 * FR
BLK = D // 128
UROWS = UNIT * BLK + 16
LANES = 8 * FR
RING = 32
NB = 16
SUB = 3
CUTS = (0, 192, 384, 592)
LOSS_SCALE = 16.0
LOG2E = math.log2(math.e)
C0 = 1.0 / (math.sqrt(FR) * math.sqrt(D))
F32 = jnp.float32
BF16 = jnp.bfloat16
MESH = pl.DeviceIdType.MESH


def ring_pos(z, x):
    u = (z - 3 * x + 24) % 8
    return (4 * z + (x + z) % 4, 4 * x + 16 * (u // 4) + u % 4)


def ring_chip(k, i):
    if k == 0:
        z = i // 4
        return z * 4 + (i % 4 - z + 8) % 4
    j = i // 4
    return ((3 * j + i % 4) % 8) * 4 + j % 4


def dot_nn(a, b):
    return jnp.dot(a, b, preferred_element_type=F32)


def dot_nt(a, b):
    return lax.dot_general(a, b, (((1,), (1,)), ((), ())), preferred_element_type=F32)


def dot_tn(a, b):
    return lax.dot_general(a, b, (((0,), (0,)), ((), ())), preferred_element_type=F32)


def col_softmax(scores):
    scale = LOG2E / math.sqrt(D)
    top = jnp.max(scores, axis=0, keepdims=True)
    e = jnp.exp2((scores - top) * scale)
    return e * (1.0 / jnp.sum(e, axis=0, keepdims=True))


def batch_scores(peer, own_t, own_st):
    scores_x = dot_nn(peer, own_t)
    by_peer = jnp.concatenate(
        [col_softmax(scores_x[p * FR : (p + 1) * FR]) for p in range(8)], axis=0
    )
    by_peer = by_peer.T.astype(BF16)
    return by_peer, dot_nt(own_st, peer)


def batch_terms(by_peer, both, seg, weights, signs):
    total, first, second, z1s = [], [], [], []
    for a in range(8):
        rows = slice(a * FR, (a + 1) * FR)
        t = both[OWN2 + a * FR : OWN2 + (a + 1) * FR]
        p1 = by_peer[rows].astype(F32)
        p2 = col_softmax(both[rows]).astype(BF16).astype(F32)
        z1 = p1 * t
        z2 = p2 * t
        r2 = jnp.sum(z2, axis=0, keepdims=True)
        total.append(jnp.sum(z1, axis=0, keepdims=True) + r2)
        z1s.append(z1.astype(BF16))
        first.append(p1 + p2)
        second.append((z1 + z2 - p2 * r2, p1))
    sums = jnp.concatenate(total, axis=0)
    high = sums.astype(BF16)
    low = (sums - high.astype(F32)).astype(BF16)
    spread = dot_nn(jnp.concatenate([high, low], axis=0), seg)
    logit = (spread[:8] + spread[8:]) * C0
    coef = weights * signs * (-LOSS_SCALE * C0) / (1.0 + jnp.exp(signs * logit))
    r1 = dot_nn(jnp.concatenate(z1s, axis=0), seg)
    out1, out2 = [], []
    for a in range(8):
        c = coef[a : a + 1]
        g, p1 = second[a]
        out1.append((c * first[a]).astype(BF16))
        out2.append((c * (g - p1 * r1[a * FR : (a + 1) * FR])).astype(BF16))
    return jnp.concatenate(out1 + out2, axis=0)


FLAT = BLK * D
HALF = FLAT // 2
QUARTER = HALF // 4
PIECE = QUARTER // 4
N_COPIES = 4 + 2 + 6 + 6 + 14 + 3 + 3 + 1


def kernel(
    x_ref, gain_ref, w_ref, v_ref, left_ref, right_ref, clique_ref,
    gf_ref, out_ref, score_ref,
    buf, own8, own_st, own_t, hid, hid_t, cnt, seg, ind_m, sel, small, terms, acc,
    give, got,
    flat, rc, sx, rx, sy, ry, rz, full, tc, tx, ty, tz,
    ssem, rsem, sems, rems,
):
    y = lax.axis_index("grp")
    me = lax.axis_index("dev")
    core = me % 2
    chip = me // 2
    x = chip % 4
    z = chip // 4
    pos = ring_pos(z, x)
    near = [
        [(y, ring_chip(k, (pos[k] + step) % RING) * 2 + core) for k in range(2)]
        for step in (1, RING - 1)
    ]
    sib_dev = me + 1 - 2 * core
    sib = (y, sib_dev)
    along_x = [(y, (z * 4 + (x + s) % 4) * 2 + core) for s in range(1, 4)]
    along_y = [((y + s) % 4, me) for s in range(1, 4)]
    along_z = [(y, (((z + s) % 8) * 4 + x) * 2 + core) for s in range(1, 8)]

    barrier = pltpu.get_barrier_semaphore()
    for dev in [sib] + along_x + along_y + along_z:
        pl.semaphore_signal(barrier, inc=1, device_id=dev, device_id_type=MESH)

    def ring(sb, su, db, du, dev, s):
        part = pl.ds(CUTS[s], CUTS[s + 1] - CUTS[s])
        return pltpu.make_async_remote_copy(
            src_ref=buf.at[sb, su, part],
            dst_ref=buf.at[db, du, part],
            send_sem=ssem.at[db, du * SUB + s],
            recv_sem=rsem.at[db, du * SUB + s],
            device_id=dev,
            device_id_type=MESH,
        )

    count = [0]
    pending = []

    def remote(src, dst, dev):
        i = count[0]
        count[0] += 1
        copy = pltpu.make_async_remote_copy(
            src_ref=src, dst_ref=dst, send_sem=sems.at[i], recv_sem=rems.at[i],
            device_id=dev, device_id_type=MESH,
        )
        copy.start()
        pending.append(copy)
        return copy

    def rows(start, size):
        return pl.ds(pl.multiple_of(start, 16), size)

    def ids(shape, dim):
        return lax.broadcasted_iota(jnp.int32, shape, dim)

    def mark(cond):
        return jnp.where(cond, 1.0, 0.0).astype(BF16)

    values = x_ref[...].astype(F32)
    square_mean = jnp.mean(values * values, axis=-1, keepdims=True)
    hidden = (values * lax.rsqrt(square_mean + 1e-06) * gain_ref[...]).astype(BF16)
    feats = (values + dot_nn(hidden, w_ref[...])).astype(BF16)
    hot_left = mark(ids((16, 128), 0) == left_ref[...])
    hot_right = mark(ids((256, 128), 0) == right_ref[...] - y * 256)
    counts = dot_nt(hot_left, hot_right)
    for k in range(2):
        for j in range(BLK):
            buf[NB - 1, 2 + k, j * UNIT : (j + 1) * UNIT, :] = feats[
                k * UNIT : (k + 1) * UNIT, j * 128 : (j + 1) * 128
            ]
        lines = [
            counts[2 * k + l : 2 * k + l + 1, h * 128 : (h + 1) * 128]
            for l in range(2)
            for h in range(2)
        ]
        buf[NB - 1, 2 + k, BLK * UNIT : UROWS, :] = jnp.concatenate(
            lines + [jnp.zeros((12, 128), F32)], axis=0
        ).astype(BF16)
    own8[:OWN] = feats
    hid[:OWN] = hidden
    cnt[0] = counts.astype(BF16)

    pl.semaphore_wait(barrier, 14)
    for s in range(SUB):
        for k in range(2):
            for way in range(2):
                ring(NB - 1, 2 + k, 0, way * 2 + k, near[way][k], s).start()
    fcopy = remote(own8.at[pl.ds(0, OWN)], own8.at[pl.ds(OWN, OWN)], sib)
    ccopy = remote(cnt.at[0], cnt.at[1], sib)
    hcopy = remote(hid.at[pl.ds(0, OWN)], hid.at[pl.ds(OWN, OWN)], sib)

    shape = (LANES, LANES)
    seg[...] = mark(ids(shape, 0) // FR == ids(shape, 1) // FR)
    shape = (64, LANES)
    row = ids(shape, 0)
    song = 2 * (row // 16) + (row % 16) // 2
    right_row = jnp.logical_and(row % 16 < 4, row % 2 == me // 32)
    ind_m[...] = mark(jnp.logical_and(right_row, song == ids(shape, 1) // FR))
    shape = (16, 128)
    row = ids(shape, 0)
    own_song = jnp.where(row < 4, (me % 32) * 4 + row, (sib_dev % 32) * 4 + row - 4)
    chosen = jnp.logical_and(row < 8, ids(shape, 1) == own_song)
    sel[...] = mark(chosen)
    acc[...] = jnp.zeros_like(acc)
    terms[...] = jnp.zeros_like(terms)

    shape = (256, 128)
    lane = ids((1, 128), 1)
    t = lane // 8 + 1
    u = (lane % 8) // 2
    k = u % 2
    last = jnp.logical_and(t == NB, u >= 2)
    shift = jnp.where(last, 0, jnp.where(u >= 2, t, RING - t))
    origin = jnp.where(
        k == 0, ring_chip(0, (pos[0] + shift) % RING), ring_chip(1, (pos[1] + shift) % RING)
    )
    landing = (origin * 2 + core) * 4 + 2 * k + lane % 2
    hot = mark(ids(shape, 0) == landing)
    group_rows = [clique_ref[pl.ds(2 * y + h, 1), :] for h in range(2)]
    theirs = jnp.concatenate(group_rows, axis=1).astype(F32)
    near_row = clique_ref[pl.ds(2 * y + me // 32, 1), :].astype(F32)
    mine = jnp.sum(jnp.where(chosen, near_row, 0.0), axis=1, keepdims=True)[:8]
    signs = jnp.where(mine == theirs, 1.0, -1.0)
    fcopy.wait_recv()
    ccopy.wait_recv()
    table = jnp.concatenate(
        [cnt[0].astype(F32)[:4], cnt[1].astype(F32)[:4], signs], axis=0
    ).astype(BF16)
    small[...] = dot_nn(table, hot).astype(BF16)
    feats8 = own8[...]
    own_st[:OWN2] = feats8
    own_st[OWN2:] = (feats8.astype(F32) * v_ref[...]).astype(BF16)
    own_t[...] = feats8.T

    def peer_of(b):
        return jnp.concatenate(
            [
                buf[b, :, j * UNIT : (j + 1) * UNIT, :].reshape(LANES, 128)
                for j in range(BLK)
            ],
            axis=1,
        )

    def step(b, carry):
        for s in range(SUB):
            for u in range(4):

                def hop():
                    ring(b, u, b, u, sib, s).wait_recv()
                    way = near[u // 2][u % 2]

                    @pl.when(b < (NB - 1 if u < 2 else NB - 2))
                    def _():
                        ring(b, u, b + 1, u, way, s).start()

                if u < 2:
                    hop()
                else:
                    pl.when(b < NB - 1)(hop)

        peer = peer_of(b)
        by_peer, both = batch_scores(peer, own_t[...], own_st[...])

        acc[...] += dot_nn(terms[...], peer_of(jnp.maximum(b - 1, 0)))
        meta = buf[b, :, BLK * UNIT : UROWS, :].reshape(64, 128)
        lanes = ids((128, LANES), 1) // FR
        wexp = dot_nn(small[...], mark(ids((128, LANES), 0) == lanes + 8 * b))
        right = dot_nn(dot_nt(sel[...], meta).astype(BF16), ind_m[...])
        terms[...] = batch_terms(by_peer, both, seg[...], wexp[:8] + right[:8], wexp[8:])
        return carry

    lax.fori_loop(0, NB, step, 0)
    acc[...] += dot_nn(terms[...], peer_of(NB - 1))

    first = acc[:OWN2]
    grads = v_ref[...] * first + acc[OWN2:] * (1.0 / math.sqrt(D))
    give[...] = grads[OWN:].astype(BF16)
    gcopy = remote(give, got, sib)
    high = grads.astype(BF16)
    hcopy.wait_recv()
    hid_t[...] = hid[...].T
    for j in range(BLK):
        part = dot_nn(hid_t[...], high[:, j * 128 : (j + 1) * 128])
        flat[j * D : (j + 1) * D, :] = part.astype(BF16)
    a = remote(flat.at[rows((1 - core) * HALF, HALF)], rc, sib)
    score = 0.5 * jnp.sum(own_st[:OWN2].astype(F32) * first, axis=0, keepdims=True)
    score = jnp.concatenate(
        [score[:, j * 128 : (j + 1) * 128] for j in range(BLK)]
        + [jnp.zeros((8 - BLK, 128), F32)],
        axis=0,
    )
    tc[core] = score
    b = remote(tc.at[core], tc.at[core], sib)
    gcopy.wait_recv()
    gf_ref[...] = grads[:OWN] + got[...].astype(F32)
    a.wait_recv()
    b.wait_recv()
    sx[...] = (
        flat[rows(core * HALF, HALF), :].astype(F32) + rc[...].astype(F32)
    ).astype(BF16)
    tx[x] = tc[0] + tc[1]

    copies = []
    for s, dev in enumerate(along_x):
        to = (x + s + 1) % 4
        copies.append(remote(sx.at[rows(to * QUARTER, QUARTER)], rx.at[s], dev))
        copies.append(remote(tx.at[x], tx.at[x], dev))
    for c in copies:
        c.wait_recv()
    sy[...] = (
        sx[rows(x * QUARTER, QUARTER), :].astype(F32)
        + rx[0].astype(F32)
        + rx[1].astype(F32)
        + rx[2].astype(F32)
    ).astype(BF16)
    ty[y] = (tx[0] + tx[1]) + (tx[2] + tx[3])

    copies = []
    for s, dev in enumerate(along_y):
        to = (y + s + 1) % 4
        copies.append(remote(sy.at[rows(to * PIECE, PIECE)], ry.at[s], dev))
        copies.append(remote(ty.at[y], ty.at[y], dev))
    for c in copies:
        c.wait_recv()
    rz[z] = (
        sy[rows(y * PIECE, PIECE), :].astype(F32)
        + ry[0].astype(F32)
        + ry[1].astype(F32)
        + ry[2].astype(F32)
    ).astype(BF16)
    tz[z] = (ty[0] + ty[1]) + (ty[2] + ty[3])

    copies = []
    for dev in along_z:
        copies.append(remote(rz.at[z], rz.at[z], dev))
        copies.append(remote(tz.at[z], tz.at[z], dev))
    for c in copies:
        c.wait_recv()
    total = rz[0].astype(F32)
    score = tz[0]
    for i in range(1, 8):
        total = total + rz[i].astype(F32)
        score = score + tz[i]
    score_ref[...] = score
    first = core * HALF + x * QUARTER
    mine = rows(first + y * PIECE, PIECE)
    full[mine, :] = total.astype(BF16)

    copies = [remote(full.at[mine], full.at[mine], dev) for dev in along_y]
    for c in copies:
        c.wait_recv()
    quarter = rows(first, QUARTER)
    copies = [remote(full.at[quarter], full.at[quarter], dev) for dev in along_x]
    for c in copies:
        c.wait_recv()
    half = rows(core * HALF, HALF)
    remote(full.at[half], full.at[half], sib).wait_recv()
    for j in range(BLK):
        out_ref[:, j * 128 : (j + 1) * 128] = full[j * D : (j + 1) * D, :]
    for c in pending:
        c.wait_send()

    def drain(b, carry):
        for s in range(SUB):
            for u in range(4):

                def done():
                    ring(b, u, b, u, sib, s).wait_send()

                if u < 2:
                    done()
                else:
                    pl.when(b < NB - 1)(done)
        return carry

    lax.fori_loop(0, NB, drain, 0)


def local(songs, gain, enc_weight, score_vec, left_local, right_song, clique):
    vmem = pl.BlockSpec(memory_space=pltpu.VMEM)
    gf, weight, total = pl.pallas_call(
        kernel,
        out_shape=(
            jax.ShapeDtypeStruct((OWN, D), F32),
            jax.ShapeDtypeStruct((D, D), BF16),
            jax.ShapeDtypeStruct((8, 128), F32),
        ),
        in_specs=[vmem] * 7,
        out_specs=(vmem,) * 3,
        scratch_shapes=[
            pltpu.VMEM((NB, 4, UROWS, 128), BF16),
            pltpu.VMEM((OWN2, D), BF16),
            pltpu.VMEM((2 * OWN2, D), BF16),
            pltpu.VMEM((D, OWN2), BF16),
            pltpu.VMEM((OWN2, D), BF16),
            pltpu.VMEM((D, OWN2), BF16),
            pltpu.VMEM((2, 16, 256), BF16),
            pltpu.VMEM((LANES, LANES), BF16),
            pltpu.VMEM((64, LANES), BF16),
            pltpu.VMEM((16, 128), BF16),
            pltpu.VMEM((16, 128), BF16),
            pltpu.VMEM((2 * OWN2, LANES), BF16),
            pltpu.VMEM((2 * OWN2, D), F32),
            pltpu.VMEM((OWN, D), BF16),
            pltpu.VMEM((OWN, D), BF16),
            pltpu.VMEM((FLAT, 128), BF16),
            pltpu.VMEM((HALF, 128), BF16),
            pltpu.VMEM((HALF, 128), BF16),
            pltpu.VMEM((3, QUARTER, 128), BF16),
            pltpu.VMEM((QUARTER, 128), BF16),
            pltpu.VMEM((3, PIECE, 128), BF16),
            pltpu.VMEM((8, PIECE, 128), BF16),
            pltpu.VMEM((FLAT, 128), BF16),
            pltpu.VMEM((2, 8, 128), F32),
            pltpu.VMEM((4, 8, 128), F32),
            pltpu.VMEM((4, 8, 128), F32),
            pltpu.VMEM((8, 8, 128), F32),
            pltpu.SemaphoreType.DMA((NB, 4 * SUB)),
            pltpu.SemaphoreType.DMA((NB, 4 * SUB)),
            pltpu.SemaphoreType.DMA((N_COPIES,)),
            pltpu.SemaphoreType.DMA((N_COPIES,)),
        ],
        compiler_params=pltpu.CompilerParams(
            collective_id=0, has_side_effects=True, vmem_limit_bytes=52 * 2**20
        ),
    )(
        songs.reshape(OWN, D),
        gain.reshape(1, D),
        enc_weight,
        score_vec.reshape(1, D),
        left_local.reshape(1, 128),
        right_song.reshape(1, 128),
        clique.reshape(8, 128),
    )
    return (
        gf.reshape(4, FR, D),
        weight.astype(F32),
        total[:BLK].reshape(D),
    )


def solution(mesh):
    in_specs = (
        P(("grp", "dev"), None, None),
        P(),
        P(),
        P(),
        P(("grp", "dev")),
        P(("grp", "dev")),
        P(),
    )
    out_specs = (P(("grp", "dev"), None, None), P(), P())
    return jax.shard_map(local, mesh=mesh, in_specs=in_specs, out_specs=out_specs, check_vma=False)
```

time: 142 us -> 135 us (0.951)
  Pallas kernels: 131 us -> 125 us
    pallas_call x2 -> x1, Pallas kernels: 131 us -> 125 us  [local(): pl.pallas_call(kernel, out_shape=(jax.ShapeDtypeStruct((OWN, D), F32), ja...]
    unnamed x3 -> x9, local copies, waits for them, and re-layouts: 0.82 us -> 3.77 us
    dynamic_slice x2 -> x0, local copies, waits for them, and re-layouts: 1.52 us -> none  [clique_of(): return lax.dynamic_slice_in_dim(clique, start, size)]
where the time goes in v2:
time: 135 us
  Pallas kernels  125 us (93%)
  local copies, waits for them, and re-layouts  5.75 us (4%)
  other arithmetic  2.85 us (2%)
    pallas_call x1, Pallas kernels, local(): pl.pallas_call(kernel, out_shape=(jax.ShapeDtypeStruct((OWN, D), F32), ja...  125 us
    unnamed x9, local copies, waits for them, and re-layouts  3.77 us
    convert_element_type x1, other arithmetic, local(): return (gf.reshape(4, FR, D), weight.astype(F32), total[:BLK].reshape(D))  2.85 us

profile of v2, /device:TPU:1, one launch (start us, length us, event | category | flops | bytes accessed | tf_op | source)
XLA Modules:
  0.0 134.7 jit_solution(11863501093230323124)
XLA Ops:
  0.6 0.7 reshape.31.gain_ref
  1.3 0.7 reshape.32.v_ref
  2.0 0.0 copy-start
  2.0 1.0 copy-done
  3.0 0.0 copy-start.1
  3.0 0.7 copy-done.1
  3.7 0.0 copy-start.2
  3.7 0.7 copy-done.2
  4.3 0.0 copy-start.3
  4.3 0.7 copy-done.3
  5.0 125.5 %shard_map.94 = (f32[192,768]{1,0:T(8,128)S(1)}, bf16[768,768]{1,0:T(8,128)(2,1)}, f32[8,128]{1,0:T(8,128)S(1)}) custom-call(bf16[192,768]{1,0:T(8,128)(2,1)S(1)} %bitcast.8, f32[1,768]{1,0:T(1,128)S(1)} %reshape.31.gain_ref, bf16[768,768]{1,0:T(8,128)(2,1)} %w_ref.1, f32[1,768]{1,0:T(1,128)S(1)} %reshape.32.v_ref, s32[1,128]{1,0:T(1,128)S(1)} %bitcast.10, ...), custom_call_target="tpu_custom_call" | custom-call | tf_op jit(solution)/shard_map/pallas_call | solution.py:394
  130.5 0.6 slice_bitcast_fusion
  131.1 2.8 %convert_element_type.3 = f32[768,768]{1,0:T(8,128)} convert(bf16[768,768]{1,0:T(8,128)(2,1)} %get-tuple-element.7) | non-fusion elementwise | flops 589824 | bytes 3538944 | tf_op jit(solution)/shard_map/convert_element_type | solution.py:450
  133.9 0.8 copy.11
Async XLA Ops:
  2.0 1.0 copy-start
  3.0 0.7 copy-start.1
  3.7 0.7 copy-start.2
  4.3 0.7 copy-start.3

commit v3 on v2

v3 whole, which is shorter than its diff:
```python
import functools
import math

import jax
import jax.numpy as jnp
from jax import lax
from jax.experimental import pallas as pl
from jax.experimental.pallas import tpu as pltpu
from jax.sharding import PartitionSpec as P

D = 768
FR = 48
OWN = 4 * FR
GRP = 2 * OWN
UNIT = 2 * FR
BLK = D // 128
UROWS = UNIT * BLK + 16
LANES = 8 * FR
NB = 8
STEPS = 2 * NB
POLLS = ((1, 1), (2, 2), (4, 3), (6, 4), (8, 5), (10, 6), (14, 7))
FAR = (0, 0, 1, 3, 1, 3, 2, 2)
PART = (0, 1, 1, 0, 0, 1, 0, 1)
LOSS_SCALE = 16.0
LOG2E = math.log2(math.e)
C0 = 1.0 / (math.sqrt(FR) * math.sqrt(D))
F32 = jnp.float32
BF16 = jnp.bfloat16
MESH = pl.DeviceIdType.MESH


def dot_nn(a, b):
    return jnp.dot(a, b, preferred_element_type=F32)


def dot_nt(a, b):
    return lax.dot_general(a, b, (((1,), (1,)), ((), ())), preferred_element_type=F32)


def dot_tn(a, b):
    return lax.dot_general(a, b, (((0,), (0,)), ((), ())), preferred_element_type=F32)


def col_softmax(scores):
    scale = LOG2E / math.sqrt(D)
    top = jnp.max(scores, axis=0, keepdims=True)
    e = jnp.exp2((scores - top) * scale)
    return e * (1.0 / jnp.sum(e, axis=0, keepdims=True))


def batch_scores(peer, own_t):
    st = dot_nn(peer, own_t)
    scores_x = st[:, :GRP]
    ps, gs = [], []
    for p in range(8):
        prob = col_softmax(scores_x[p * FR : (p + 1) * FR]).astype(BF16)
        pf = prob.astype(F32)
        prod = st[p * FR : (p + 1) * FR, GRP:]
        zz = pf * prod
        ps.append(prob)
        gs.append((zz - pf * jnp.sum(zz, axis=0, keepdims=True)).astype(BF16))
    by_peer = jnp.concatenate(ps, axis=0).T
    grad_peer = jnp.concatenate(gs, axis=0).T
    return by_peer, grad_peer, st.T


def batch_terms(by_peer, grad_peer, both, seg, weights, signs):
    total, first, second, z1s = [], [], [], []
    for a in range(8):
        rows = slice(a * FR, (a + 1) * FR)
        t = both[GRP + a * FR : GRP + (a + 1) * FR]
        p1 = by_peer[rows].astype(F32)
        p2 = col_softmax(both[rows]).astype(BF16).astype(F32)
        z2 = p2 * t
        r2 = jnp.sum(z2, axis=0, keepdims=True)
        total.append(jnp.sum(p1 * t, axis=0, keepdims=True) + r2)
        first.append(p1 + p2)
        second.append(z2 - p2 * r2 + grad_peer[rows].astype(F32))
    sums = jnp.concatenate(total, axis=0)
    high = sums.astype(BF16)
    low = (sums - high.astype(F32)).astype(BF16)
    spread = dot_nn(jnp.concatenate([high, low], axis=0), seg)
    logit = (spread[:8] + spread[8:]) * C0
    coef = weights * signs * (-LOSS_SCALE * C0) / (1.0 + jnp.exp(signs * logit))
    out1, out2 = [], []
    for a in range(8):
        c = coef[a : a + 1]
        out1.append((c * first[a]).astype(BF16))
        out2.append((c * second[a]).astype(BF16))
    return jnp.concatenate(out1 + out2, axis=0)


CHUNKS = 2
PIECE = 80
CORE = 16 * PIECE
CHUNK = 2 * CORE
FLAT = CHUNKS * CHUNK
WEIGHT = BLK * D
N_COPIES = 3 + 6 + CHUNKS * (1 + 15 + 7 + 15 + 1)


def kernel(
    x_hbm, gain_hbm, w_hbm, v_hbm, left_hbm, right_hbm, clique_hbm,
    gf_ref, out_ref, score_ref,
    x_ref, gain_ref, w_ref, v_ref, left_ref, right_ref, clique_ref, in_sems,
    xin, buf, own_st, own_t, hid, hid_t, cnt, seg, ind_m, sel, small, terms, acc,
    give, back,
    flat, rc, half, rp, rz, full,
    csend, crecv, xsend, xrecv, sems, rems,
):
    y = lax.axis_index("grp")
    me = lax.axis_index("dev")
    core = me % 2
    chip = me // 2
    x = chip % 4
    z = chip // 4
    sib = (y, me + 1 - 2 * core)
    along_x = [(y, (z * 4 + (x + s) % 4) * 2 + core) for s in range(1, 4)]
    along_z = [(y, (((z + s) % 8) * 4 + x) * 2 + core) for s in range(1, 8)]
    spread = [(sy, sx) for sy in range(4) for sx in range(4) if sy or sx]
    plane = [((y + sy) % 4, (z * 4 + (x + sx) % 4) * 2 + core) for sy, sx in spread]
    x_up, x_far, x_down = along_x
    z_up, z_down = along_z[0], along_z[6]

    inputs = [
        pltpu.make_async_copy(src, dst, in_sems.at[n])
        for n, (src, dst) in enumerate(
            (
                (x_hbm, x_ref),
                (left_hbm, left_ref),
                (right_hbm, right_ref),
                (w_hbm, w_ref),
                (gain_hbm, gain_ref),
                (v_hbm, v_ref),
                (clique_hbm, clique_ref),
            )
        )
    ]
    for copy in inputs:
        copy.start()
    barrier = pltpu.get_barrier_semaphore()
    for dev in [sib] + plane + along_z:
        pl.semaphore_signal(barrier, inc=1, device_id=dev, device_id_type=MESH)

    def column(sb, su, db, du, dev):
        return pltpu.make_async_remote_copy(
            src_ref=buf.at[sb, su], dst_ref=buf.at[db, du],
            send_sem=csend.at[db, du], recv_sem=crecv.at[db, du],
            device_id=dev, device_id_type=MESH,
        )

    def row_unit(src, dst, dev):
        return pltpu.make_async_remote_copy(
            src_ref=xin.at[src], dst_ref=xin.at[dst],
            send_sem=xsend.at[dst], recv_sem=xrecv.at[dst],
            device_id=dev, device_id_type=MESH,
        )

    count = [0]
    pending = []

    def remote(src, dst, dev):
        i = count[0]
        count[0] += 1
        copy = pltpu.make_async_remote_copy(
            src_ref=src, dst_ref=dst, send_sem=sems.at[i], recv_sem=rems.at[i],
            device_id=dev, device_id_type=MESH,
        )
        copy.start()
        pending.append(copy)
        return copy

    def rows(start, size):
        return pl.ds(pl.multiple_of(start, 16), size)

    def ids(shape, dim):
        return lax.broadcasted_iota(jnp.int32, shape, dim)

    def mark(cond):
        return jnp.where(cond, 1.0, 0.0).astype(BF16)

    for copy in inputs[:3]:
        copy.wait()
    for k in range(2):
        xin[k] = x_ref[k * UNIT : (k + 1) * UNIT]
    hot_left = mark(ids((16, 128), 0) == left_ref[...])
    hot_right = mark(ids((256, 128), 0) == right_ref[...] - y * 256)
    counts = dot_nt(hot_left, hot_right)
    cnt[0] = counts.astype(BF16)
    pl.semaphore_wait(barrier, 23)
    row_unit(1, 2, x_down).start()
    row_unit(0, 3, x_up).start()
    row_unit(0, 4, x_down).start()
    row_unit(1, 5, x_up).start()
    tables = [remote(cnt.at[0], cnt.at[3 - s], dev) for s, dev in enumerate(along_x)]

    for copy in inputs[3:]:
        copy.wait()

    def wide(ref):
        return jnp.concatenate([ref[j : j + 1, :] for j in range(BLK)], axis=1)

    gain = wide(gain_ref)
    score_vec = wide(v_ref)

    def encode(songs):
        values = songs.astype(F32)
        square_mean = jnp.mean(values * values, axis=-1, keepdims=True)
        hidden = (values * lax.rsqrt(square_mean + 1e-06) * gain).astype(BF16)
        feats = (values + dot_nn(hidden, w_ref[...])).astype(BF16)
        return hidden, feats

    hidden, feats = encode(x_ref[...])
    hid[:OWN] = hidden
    own_st[0, :OWN] = feats
    for k in range(2):
        for j in range(BLK):
            buf[0, k, j * UNIT : (j + 1) * UNIT, :] = feats[
                k * UNIT : (k + 1) * UNIT, j * 128 : (j + 1) * 128
            ]
        lines = [
            counts[2 * k + l : 2 * k + l + 1, h * 128 : (h + 1) * 128]
            for l in range(2)
            for h in range(2)
        ]
        buf[0, k, BLK * UNIT : UROWS, :] = jnp.concatenate(
            lines + [jnp.zeros((12, 128), F32)], axis=0
        ).astype(BF16)
    for k in range(2):
        column(0, k, 1 + k, 0, z_up).start()
        column(0, k, 1 + k, 1, z_down).start()
        column(0, k, 0, 2 + k, sib).start()

    shape = (LANES, LANES)
    seg[...] = mark(ids(shape, 0) // FR == ids(shape, 1) // FR)
    shape = (64, LANES)
    row = ids(shape, 0)
    song = 2 * (row // 16) + (row % 16) // 2
    right_row = jnp.logical_and(row % 16 < 4, row % 2 == z // 4)
    ind_m[...] = mark(jnp.logical_and(right_row, song == ids(shape, 1) // FR))
    acc[...] = jnp.zeros_like(acc)
    terms[...] = jnp.zeros_like(terms)

    lane = ids((1, 128), 1)
    b = lane // 8
    u = (lane % 8) // 2
    way = u % 2
    t = (b + 1) // 2
    dz = jnp.where(b == 0, 0, jnp.where(way == 0, 8 - t % 8, t))
    k = jnp.where(jnp.logical_or(b == 0, b == NB - 1), way, (b + 1) % 2)
    held = (((z + dz) % 8) * 4 + x) * 2 + jnp.where(u < 2, core, 1 - core)
    landing = held * 4 + 2 * k + lane % 2
    hot = mark(ids((256, 128), 0) == landing)
    group_rows = [clique_ref[pl.ds(2 * y + h, 1), :] for h in range(2)]
    theirs = jnp.concatenate(group_rows, axis=1).astype(F32)
    near_row = clique_ref[pl.ds(2 * y + z // 4, 1), :].astype(F32)
    for copy in tables:
        copy.wait_recv()
    for r in range(2):
        shape = (16, 128)
        row = ids(shape, 0)
        number = row * 0 - 1
        for w in range(4):
            first = ((z % 4) * 4 + (x + FAR[4 * r + w]) % 4) * 8 + core * 4 + 2 * PART[4 * r + w]
            number = jnp.where(row // 2 == w, first + row % 2, number)
        chosen = ids(shape, 1) == number
        sel[r] = mark(chosen)
        mine = jnp.sum(jnp.where(chosen, near_row, 0.0), axis=1, keepdims=True)[:8]
        signs = jnp.where(mine == theirs, 1.0, -1.0)
        left = [
            cnt[FAR[4 * r + w]].astype(F32)[2 * PART[4 * r + w] : 2 * PART[4 * r + w] + 2]
            for w in range(4)
        ]
        table = jnp.concatenate(left + [signs], axis=0).astype(BF16)
        small[r] = dot_nn(table, hot).astype(BF16)

    def prepare(r):
        feats = own_st[r, :GRP]
        own_st[r, GRP:] = (feats.astype(F32) * score_vec).astype(BF16)
        own_t[r] = own_st[r].T

    def arrived(b, u):
        column(b, u, b, u, sib).wait_recv()

    for u in (2, 3):
        row_unit(u, u, x_up).wait_recv()
    row_unit(3, 6, x_up).start()
    row_unit(2, 7, x_down).start()
    hidden, feats = encode(xin[2:4].reshape(OWN, D))
    hid[OWN:GRP] = hidden
    own_st[0, OWN:GRP] = feats
    prepare(0)

    def peer_of(b):
        return jnp.concatenate(
            [
                buf[b, :, j * UNIT : (j + 1) * UNIT, :].reshape(LANES, 128)
                for j in range(BLK)
            ],
            axis=1,
        )

    def order(i):
        late = (i + 10) // 16
        return (
            (1 - late) * (i % 3) + late * (i // 2),
            (1 - late) * (i // 3) + late * ((i + i // 14) % 2),
        )

    def step(i, carry):
        b, r = order(i)

        for at, ahead in POLLS:

            @pl.when(i == at)
            def _():
                for way, dev in ((0, z_up), (1, z_down)):
                    arrived(ahead, way)
                    if ahead < 5:
                        column(ahead, way, ahead + 2, way, dev).start()
                    elif ahead == 5 + way:
                        column(ahead, way, 7, way, dev).start()
                    column(ahead, way, ahead, 2 + way, sib).start()

        @pl.when(i == 3)
        def _():
            for u in (4, 5, 6, 7):
                row_unit(u, u, x_up).wait_recv()
            hidden, feats = encode(xin[4:8].reshape(GRP, D))
            hid[GRP:] = hidden
            own_st[1, :GRP] = feats
            prepare(1)
            hid_t[...] = hid[...].T

        @pl.when(jnp.logical_or(i < 3, jnp.logical_and(i >= 6, i % 2 == 0)))
        def _():
            for k in range(2):
                arrived(b, 2 + k)

        peer = peer_of(b)
        by_peer, grad_peer, both = batch_scores(peer, own_t[r])

        before, rows_before = order(jnp.maximum(i - 1, 0))
        acc[rows_before] += dot_nn(terms[...], peer_of(before))
        meta = buf[b, :, BLK * UNIT : UROWS, :].reshape(64, 128)
        lanes = ids((128, LANES), 1) // FR
        wexp = dot_nn(small[r], mark(ids((128, LANES), 0) == lanes + 8 * b))
        right = dot_nn(dot_nt(sel[r], meta).astype(BF16), ind_m[...])
        terms[...] = batch_terms(
            by_peer, grad_peer, both, seg[...], wexp[:8] + right[:8], wexp[8:]
        )
        return carry

    lax.fori_loop(0, STEPS, step, 0)
    acc[0] += dot_nn(terms[...], peer_of(NB - 1))

    score = jnp.zeros((1, D), F32)
    for r in range(2):
        first = acc[r, :GRP]
        grads = score_vec * first + acc[r, GRP:] * (1.0 / math.sqrt(D))
        if r == 0:
            gf_ref[...] = grads[:OWN]
        give[4 * r : 4 * r + 4] = grads.astype(BF16).reshape(4, UNIT, D)
        score += 0.5 * jnp.sum(own_st[r, :GRP].astype(F32) * first, axis=0, keepdims=True)
    for j in range(BLK):
        high = give[:, :, j * 128 : (j + 1) * 128].reshape(2 * GRP, 128)
        flat[j * D : (j + 1) * D, :] = dot_nn(hid_t[...], high).astype(BF16)
    flat[WEIGHT : WEIGHT + 16, :] = jnp.concatenate(
        [score[:, j * 128 : (j + 1) * 128] for j in range(BLK)]
        + [jnp.zeros((16 - BLK, 128), F32)],
        axis=0,
    ).astype(BF16)
    flat[WEIGHT + 16 :, :] = jnp.zeros((FLAT - WEIGHT - 16, 128), BF16)

    chunks = range(CHUNKS)
    copies = [
        remote(flat.at[rows(h * CHUNK + (1 - core) * CORE, CORE)], rc.at[h], sib)
        for h in chunks
    ]
    plane_copies = []
    for h in chunks:
        copies[h].wait_recv()
        half[h] = (
            flat[rows(h * CHUNK + core * CORE, CORE), :].astype(F32) + rc[h].astype(F32)
        ).astype(BF16)
        plane_copies.append(
            [
                remote(
                    half.at[h, rows((((y + sy) % 4) * 4 + (x + sx) % 4) * PIECE, PIECE)],
                    rp.at[h, n],
                    plane[n],
                )
                for n, (sy, sx) in enumerate(spread)
            ]
        )
    returned = []
    for k in range(2):
        returned.append(remote(give.at[(4, 2)[k]], back.at[k], x_up))
        returned.append(remote(give.at[(3, 5)[k]], back.at[2 + k], x_down))
    for k in range(2):
        returned.append(remote(give.at[6 + k], back.at[4 + k], x_far))
    line_copies = []
    for h in chunks:
        for c in plane_copies[h]:
            c.wait_recv()
        total = half[h, rows((y * 4 + x) * PIECE, PIECE), :].astype(F32)
        for n in range(15):
            total = total + rp[h, n].astype(F32)
        rz[h, z] = total.astype(BF16)
        line_copies.append([remote(rz.at[h, z], rz.at[h, z], dev) for dev in along_z])
    plane_copies = []
    for h in chunks:
        for c in line_copies[h]:
            c.wait_recv()
        total = rz[h, 0].astype(F32)
        for n in range(1, 8):
            total = total + rz[h, n].astype(F32)
        mine = rows(h * CHUNK + core * CORE + (y * 4 + x) * PIECE, PIECE)
        full[mine, :] = total.astype(BF16)
        plane_copies.append([remote(full.at[mine], full.at[mine], dev) for dev in plane])
    copies = []
    for h in chunks:
        for c in plane_copies[h]:
            c.wait_recv()
        same = rows(h * CHUNK + core * CORE, CORE)
        copies.append(remote(full.at[same], full.at[same], sib))
    for copy in returned:
        copy.wait_recv()
    for k in range(2):
        part = slice(k * UNIT, (k + 1) * UNIT)
        gf_ref[part, :] = (
            (gf_ref[part, :] + back[k].astype(F32))
            + (back[2 + k].astype(F32) + back[4 + k].astype(F32))
        )
    for c in copies:
        c.wait_recv()
    for j in range(BLK):
        out_ref[:, j * 128 : (j + 1) * 128] = full[j * D : (j + 1) * D, :]
    score_ref[...] = full[WEIGHT : WEIGHT + 16, :].astype(F32)[:8]
    for c in pending:
        c.wait_send()
    for u in range(2, 8):
        row_unit(u, u, x_up).wait_send()
    for b in range(NB):
        for u in range(4):
            if b or u > 1:
                column(b, u, b, u, sib).wait_send()


def local(songs, gain, enc_weight, score_vec, left_local, right_song, clique):
    vmem = pl.BlockSpec(memory_space=pltpu.VMEM)
    gf, weight, total = pl.pallas_call(
        kernel,
        out_shape=(
            jax.ShapeDtypeStruct((OWN, D), F32),
            jax.ShapeDtypeStruct((D, D), BF16),
            jax.ShapeDtypeStruct((8, 128), F32),
        ),
        in_specs=[pl.BlockSpec(memory_space=pl.ANY)] * 7,
        out_specs=(vmem,) * 3,
        scratch_shapes=[
            pltpu.VMEM((OWN, D), BF16),
            pltpu.VMEM((BLK, 128), F32),
            pltpu.VMEM((D, D), BF16),
            pltpu.VMEM((BLK, 128), F32),
            pltpu.VMEM((1, 128), jnp.int32),
            pltpu.VMEM((1, 128), jnp.int32),
            pltpu.VMEM((8, 128), jnp.int32),
            pltpu.SemaphoreType.DMA((7,)),
            pltpu.VMEM((8, UNIT, D), BF16),
            pltpu.VMEM((NB, 4, UROWS, 128), BF16),
            pltpu.VMEM((2, 2 * GRP, D), BF16),
            pltpu.VMEM((2, D, 2 * GRP), BF16),
            pltpu.VMEM((2 * GRP, D), BF16),
            pltpu.VMEM((D, 2 * GRP), BF16),
            pltpu.VMEM((4, 16, 256), BF16),
            pltpu.VMEM((LANES, LANES), BF16),
            pltpu.VMEM((64, LANES), BF16),
            pltpu.VMEM((2, 16, 128), BF16),
            pltpu.VMEM((2, 16, 128), BF16),
            pltpu.VMEM((2 * GRP, LANES), BF16),
            pltpu.VMEM((2, 2 * GRP, D), F32),
            pltpu.VMEM((8, UNIT, D), BF16),
            pltpu.VMEM((6, UNIT, D), BF16),
            pltpu.VMEM((FLAT, 128), BF16),
            pltpu.VMEM((CHUNKS, CORE, 128), BF16),
            pltpu.VMEM((CHUNKS, CORE, 128), BF16),
            pltpu.VMEM((CHUNKS, 15, PIECE, 128), BF16),
            pltpu.VMEM((CHUNKS, 8, PIECE, 128), BF16),
            pltpu.VMEM((FLAT, 128), BF16),
            pltpu.SemaphoreType.DMA((NB, 4)),
            pltpu.SemaphoreType.DMA((NB, 4)),
            pltpu.SemaphoreType.DMA((8,)),
            pltpu.SemaphoreType.DMA((8,)),
            pltpu.SemaphoreType.DMA((N_COPIES,)),
            pltpu.SemaphoreType.DMA((N_COPIES,)),
        ],
        compiler_params=pltpu.CompilerParams(
            collective_id=0, has_side_effects=True, vmem_limit_bytes=60 * 2**20
        ),
    )(
        songs.reshape(OWN, D),
        gain.reshape(BLK, 128),
        enc_weight,
        score_vec.reshape(BLK, 128),
        left_local.reshape(1, 128),
        right_song.reshape(1, 128),
        clique.reshape(8, 128),
    )
    return (
        gf.reshape(4, FR, D),
        weight.astype(F32),
        total[:BLK].reshape(D),
    )


def solution(mesh):
    in_specs = (
        P(("grp", "dev"), None, None),
        P(),
        P(),
        P(),
        P(("grp", "dev")),
        P(("grp", "dev")),
        P(),
    )
    out_specs = (P(("grp", "dev"), None, None), P(), P())
    return jax.shard_map(local, mesh=mesh, in_specs=in_specs, out_specs=out_specs, check_vma=False)
```

time: 135 us -> 100 us (0.74)
  Pallas kernels: 125 us -> 94.3 us
  local copies, waits for them, and re-layouts: 5.75 us -> 2.1 us
    pallas_call x1, Pallas kernels: 125 us -> 94.3 us  [local(): pl.pallas_call(kernel, out_shape=(jax.ShapeDtypeStruct((OWN, D), F32), ja...]
    unnamed x9 -> x3, local copies, waits for them, and re-layouts: 3.77 us -> 0.82 us
    reshape x2 -> x0, local copies, waits for them, and re-layouts: 1.38 us -> none  [the longest x1 0.69 us: local(): gain.reshape(1, D)]
where the time goes in v3:
time: 100 us
  Pallas kernels  94.3 us (94%)
  other arithmetic  2.91 us (3%)
  local copies, waits for them, and re-layouts  2.1 us (2%)
    pallas_call x1, Pallas kernels, local(): pl.pallas_call(kernel, out_shape=(jax.ShapeDtypeStruct((OWN, D), F32), ja...  94.3 us
    convert_element_type x1, other arithmetic, local(): return (gf.reshape(4, FR, D), weight.astype(F32), total[:BLK].reshape(D))  2.91 us

profile of v3, /device:TPU:1, one launch (start us, length us, event | category | flops | bytes accessed | tf_op | source)
XLA Modules:
  0.0 100.0 jit_solution(1167294444341959232)
XLA Ops:
  0.6 94.3 %shard_map.94 = (f32[192,768]{1,0:T(8,128)}, bf16[768,768]{1,0:T(8,128)(2,1)}, f32[8,128]{1,0:T(8,128)}) custom-call(bf16[192,768]{1,0:T(8,128)(2,1)} %bitcast.10, f32[6,128]{1,0:T(8,128)} %bitcast.11, bf16[768,768]{1,0:T(8,128)(2,1)} %w_hbm.1, f32[6,128]{1,0:T(8,128)} %bitcast.12, s32[1,128]{1,0:T(1,128)} %bitcast.14, s32[1,128]{1,0:T(1,128)} %bitcast.15, ...), custom_call_target="tpu_custom_call" | custom-call | tf_op jit(solution)/shard_map/pallas_call | solution.py:452
  95.0 1.3 %slice_bitcast_fusion = f32[768]{0:T(1024)} fusion(f32[8,128]{1,0:T(8,128)} %get-tuple-element.8), kind=kLoop, calls=%fused_computation | loop fusion | bytes 6144 | tf_op jit(solution)/shard_map/reshape | solution.py:513
  96.2 0.0 copy-start
  96.2 2.9 %convert_element_type.3 = f32[768,768]{1,0:T(8,128)} convert(bf16[768,768]{1,0:T(8,128)(2,1)} %get-tuple-element.7) | non-fusion elementwise | flops 589824 | bytes 3538944 | tf_op jit(solution)/shard_map/convert_element_type | solution.py:512
  99.1 0.0 copy-done
  99.2 0.8 copy.11
Async XLA Ops:
  96.2 2.9 %copy-start = (f32[192,768]{1,0:T(8,128)S(1)}, f32[192,768]{1,0:T(8,128)}, u32[]{:S(2)}) copy-start(f32[192,768]{1,0:T(8,128)} %get-tuple-element.6) | copy-start | bytes 1769476

commit v4 on v3

--- a/solution.py
+++ b/solution.py
@@ -18,7 +18,7 @@
 LANES = 8 * FR
 NB = 8
 STEPS = 2 * NB
-POLLS = ((1, 1), (2, 2), (4, 3), (6, 4), (8, 5), (10, 6), (14, 7))
+POLLS = ((0, 1), (1, 2), (3, 3), (4, 4), (6, 5), (8, 6), (12, 7))
 FAR = (0, 0, 1, 3, 1, 3, 2, 2)
 PART = (0, 1, 1, 0, 0, 1, 0, 1)
 LOSS_SCALE = 16.0
@@ -150,8 +150,9 @@
         )
 
     def row_unit(src, dst, dev):
+        source = xin.at[src] if src > 1 else x_hbm.at[pl.ds(src * UNIT, UNIT)]
         return pltpu.make_async_remote_copy(
-            src_ref=xin.at[src], dst_ref=xin.at[dst],
+            src_ref=source, dst_ref=xin.at[dst],
             send_sem=xsend.at[dst], recv_sem=xrecv.at[dst],
             device_id=dev, device_id_type=MESH,
         )
@@ -179,22 +180,20 @@
     def mark(cond):
         return jnp.where(cond, 1.0, 0.0).astype(BF16)
 
-    for copy in inputs[:3]:
-        copy.wait()
-    for k in range(2):
-        xin[k] = x_ref[k * UNIT : (k + 1) * UNIT]
-    hot_left = mark(ids((16, 128), 0) == left_ref[...])
-    hot_right = mark(ids((256, 128), 0) == right_ref[...] - y * 256)
-    counts = dot_nt(hot_left, hot_right)
-    cnt[0] = counts.astype(BF16)
     pl.semaphore_wait(barrier, 23)
     row_unit(1, 2, x_down).start()
     row_unit(0, 3, x_up).start()
     row_unit(0, 4, x_down).start()
     row_unit(1, 5, x_up).start()
+    for copy in inputs[1:3]:
+        copy.wait()
+    hot_left = mark(ids((16, 128), 0) == left_ref[...])
+    hot_right = mark(ids((256, 128), 0) == right_ref[...] - y * 256)
+    counts = dot_nt(hot_left, hot_right)
+    cnt[0] = counts.astype(BF16)
     tables = [remote(cnt.at[0], cnt.at[3 - s], dev) for s, dev in enumerate(along_x)]
 
-    for copy in inputs[3:]:
+    for copy in inputs[:1] + inputs[3:]:
         copy.wait()
 
     def wide(ref):
@@ -212,7 +211,6 @@
 
     hidden, feats = encode(x_ref[...])
     hid[:OWN] = hidden
-    own_st[0, :OWN] = feats
     for k in range(2):
         for j in range(BLK):
             buf[0, k, j * UNIT : (j + 1) * UNIT, :] = feats[
@@ -231,13 +229,13 @@
         column(0, k, 1 + k, 1, z_down).start()
         column(0, k, 0, 2 + k, sib).start()
 
-    shape = (LANES, LANES)
-    seg[...] = mark(ids(shape, 0) // FR == ids(shape, 1) // FR)
-    shape = (64, LANES)
-    row = ids(shape, 0)
+    lane_song = ids((1, LANES), 1) // FR
+    for a in range(8):
+        seg[a * FR : (a + 1) * FR] = mark(ids((FR, LANES), 0) * 0 + lane_song == a)
+    row = ids((64, 1), 0)
     song = 2 * (row // 16) + (row % 16) // 2
-    right_row = jnp.logical_and(row % 16 < 4, row % 2 == z // 4)
-    ind_m[...] = mark(jnp.logical_and(right_row, song == ids(shape, 1) // FR))
+    song = jnp.where(jnp.logical_and(row % 16 < 4, row % 2 == z // 4), song, -1)
+    ind_m[...] = mark(song == lane_song)
     acc[...] = jnp.zeros_like(acc)
     terms[...] = jnp.zeros_like(terms)
 
@@ -274,22 +272,24 @@
         table = jnp.concatenate(left + [signs], axis=0).astype(BF16)
         small[r] = dot_nn(table, hot).astype(BF16)
 
-    def prepare(r):
-        feats = own_st[r, :GRP]
-        own_st[r, GRP:] = (feats.astype(F32) * score_vec).astype(BF16)
-        own_t[r] = own_st[r].T
+    def prepare(r, start, feats):
+        size = feats.shape[0]
+        scaled = (feats.astype(F32) * score_vec).astype(BF16)
+        own_st[r, start : start + size] = feats
+        own_t[r, :, start : start + size] = feats.T
+        own_t[r, :, GRP + start : GRP + start + size] = scaled.T
 
     def arrived(b, u):
         column(b, u, b, u, sib).wait_recv()
 
+    prepare(0, 0, feats)
     for u in (2, 3):
         row_unit(u, u, x_up).wait_recv()
     row_unit(3, 6, x_up).start()
     row_unit(2, 7, x_down).start()
     hidden, feats = encode(xin[2:4].reshape(OWN, D))
     hid[OWN:GRP] = hidden
-    own_st[0, OWN:GRP] = feats
-    prepare(0)
+    prepare(0, OWN, feats)
 
     def peer_of(b):
         return jnp.concatenate(
@@ -328,8 +328,7 @@
                 row_unit(u, u, x_up).wait_recv()
             hidden, feats = encode(xin[4:8].reshape(GRP, D))
             hid[GRP:] = hidden
-            own_st[1, :GRP] = feats
-            prepare(1)
+            prepare(1, 0, feats)
             hid_t[...] = hid[...].T
 
         @pl.when(jnp.logical_or(i < 3, jnp.logical_and(i >= 6, i % 2 == 0)))
@@ -343,8 +342,7 @@
         before, rows_before = order(jnp.maximum(i - 1, 0))
         acc[rows_before] += dot_nn(terms[...], peer_of(before))
         meta = buf[b, :, BLK * UNIT : UROWS, :].reshape(64, 128)
-        lanes = ids((128, LANES), 1) // FR
-        wexp = dot_nn(small[r], mark(ids((128, LANES), 0) == lanes + 8 * b))
+        wexp = dot_nn(small[r], mark(ids((128, LANES), 0) == lane_song + 8 * b))
         right = dot_nn(dot_nt(sel[r], meta).astype(BF16), ind_m[...])
         terms[...] = batch_terms(
             by_peer, grad_peer, both, seg[...], wexp[:8] + right[:8], wexp[8:]
@@ -352,16 +350,26 @@
         return carry
 
     lax.fori_loop(0, STEPS, step, 0)
-    acc[0] += dot_nn(terms[...], peer_of(NB - 1))
-
     score = jnp.zeros((1, D), F32)
-    for r in range(2):
+    returned = []
+
+    def give_back(part, slot, dev):
+        returned.append(remote(give.at[part], back.at[slot], dev))
+
+    for r in (1, 0):
+        if r == 0:
+            acc[0] += dot_nn(terms[...], peer_of(NB - 1))
         first = acc[r, :GRP]
         grads = score_vec * first + acc[r, GRP:] * (1.0 / math.sqrt(D))
         if r == 0:
             gf_ref[...] = grads[:OWN]
         give[4 * r : 4 * r + 4] = grads.astype(BF16).reshape(4, UNIT, D)
-        score += 0.5 * jnp.sum(own_st[r, :GRP].astype(F32) * first, axis=0, keepdims=True)
+        if r == 1:
+            give_back(6, 4, x_far)
+            give_back(7, 5, x_far)
+            give_back(4, 0, x_up)
+            give_back(5, 3, x_down)
+        score += 0.5 * jnp.sum(own_st[r].astype(F32) * first, axis=0, keepdims=True)
     for j in range(BLK):
         high = give[:, :, j * 128 : (j + 1) * 128].reshape(2 * GRP, 128)
         flat[j * D : (j + 1) * D, :] = dot_nn(hid_t[...], high).astype(BF16)
@@ -393,12 +401,8 @@
                 for n, (sy, sx) in enumerate(spread)
             ]
         )
-    returned = []
-    for k in range(2):
-        returned.append(remote(give.at[(4, 2)[k]], back.at[k], x_up))
-        returned.append(remote(give.at[(3, 5)[k]], back.at[2 + k], x_down))
-    for k in range(2):
-        returned.append(remote(give.at[6 + k], back.at[4 + k], x_far))
+    give_back(2, 1, x_up)
+    give_back(3, 2, x_down)
     line_copies = []
     for h in chunks:
         for c in plane_copies[h]:
@@ -436,7 +440,7 @@
         c.wait_recv()
     for j in range(BLK):
         out_ref[:, j * 128 : (j + 1) * 128] = full[j * D : (j + 1) * D, :]
-    score_ref[...] = full[WEIGHT : WEIGHT + 16, :].astype(F32)[:8]
+    score_ref[...] = full[WEIGHT : WEIGHT + 16, :].astype(F32)[:BLK]
     for c in pending:
         c.wait_send()
     for u in range(2, 8):
@@ -454,7 +458,7 @@
         out_shape=(
             jax.ShapeDtypeStruct((OWN, D), F32),
             jax.ShapeDtypeStruct((D, D), BF16),
-            jax.ShapeDtypeStruct((8, 128), F32),
+            jax.ShapeDtypeStruct((BLK, 128), F32),
         ),
         in_specs=[pl.BlockSpec(memory_space=pl.ANY)] * 7,
         out_specs=(vmem,) * 3,
@@ -469,7 +473,7 @@
             pltpu.SemaphoreType.DMA((7,)),
             pltpu.VMEM((8, UNIT, D), BF16),
             pltpu.VMEM((NB, 4, UROWS, 128), BF16),
-            pltpu.VMEM((2, 2 * GRP, D), BF16),
+            pltpu.VMEM((2, GRP, D), BF16),
             pltpu.VMEM((2, D, 2 * GRP), BF16),
             pltpu.VMEM((2 * GRP, D), BF16),
             pltpu.VMEM((D, 2 * GRP), BF16),
@@ -510,7 +514,7 @@
     return (
         gf.reshape(4, FR, D),
         weight.astype(F32),
-        total[:BLK].reshape(D),
+        total.reshape(D),
     )
 
 

time: 100 us -> 97.1 us (0.971)
  Pallas kernels: 94.3 us -> 92 us
    pallas_call x1, Pallas kernels: 94.3 us -> 92 us  [local(): pl.pallas_call(kernel, out_shape=(jax.ShapeDtypeStruct((OWN, D), F32), ja...]
    reshape x1 -> x0, local copies, waits for them, and re-layouts: 1.28 us -> none  [local(): return (gf.reshape(4, FR, D), weight.astype(F32), total[:BLK].reshape(D))]
where the time goes in v4:
time: 97.1 us; the launch traced here: 97 us
  Pallas kernels  92 us (95%)
  other arithmetic  2.91 us (3%)
  local copies, waits for them, and re-layouts  1.42 us (1%)
    pallas_call x1, Pallas kernels, local(): pl.pallas_call(kernel, out_shape=(jax.ShapeDtypeStruct((OWN, D), F32), ja...  92 us
    convert_element_type x1, other arithmetic, local(): return (gf.reshape(4, FR, D), weight.astype(F32), total.reshape(D))  2.91 us

profile of v4, /device:TPU:1, one launch (start us, length us, event | category | flops | bytes accessed | tf_op | source)
XLA Modules:
  0.0 97.0 jit_solution(3741165329798021158)
XLA Ops:
  0.6 92.0 %shard_map.94 = (f32[192,768]{1,0:T(8,128)}, bf16[768,768]{1,0:T(8,128)(2,1)}, f32[6,128]{1,0:T(8,128)}) custom-call(bf16[192,768]{1,0:T(8,128)(2,1)} %bitcast.9, f32[6,128]{1,0:T(8,128)} %bitcast.10, bf16[768,768]{1,0:T(8,128)(2,1)} %w_hbm.1, f32[6,128]{1,0:T(8,128)} %bitcast.11, s32[1,128]{1,0:T(1,128)} %bitcast.14, s32[1,128]{1,0:T(1,128)} %bitcast.15, ...), custom_call_target="tpu_custom_call" | custom-call | tf_op jit(solution)/shard_map/pallas_call | solution.py:456
  92.6 0.0 copy-start
  92.6 2.9 %convert_element_type.3 = f32[768,768]{1,0:T(8,128)} convert(bf16[768,768]{1,0:T(8,128)(2,1)} %get-tuple-element.7) | non-fusion elementwise | flops 589824 | bytes 3538944 | tf_op jit(solution)/shard_map/convert_element_type | solution.py:516
  95.5 0.0 copy-done
  95.5 0.0 copy-start.1
  95.6 0.8 copy.12
  96.4 0.0 copy-done.1
  96.4 0.6 copy.13
Async XLA Ops:
  92.6 2.9 %copy-start = (f32[192,768]{1,0:T(8,128)S(1)}, f32[192,768]{1,0:T(8,128)}, u32[]{:S(2)}) copy-start(f32[192,768]{1,0:T(8,128)} %get-tuple-element.6) | copy-start | bytes 1769476
  95.5 0.8 copy-start.1

commit v5 on v4

--- a/solution.py
+++ b/solution.py
@@ -18,7 +18,13 @@
 LANES = 8 * FR
 NB = 8
 STEPS = 2 * NB
-POLLS = ((0, 1), (1, 2), (3, 3), (4, 4), (6, 5), (8, 6), (12, 7))
+POLLS = ((0, 1), (2, 2), (3, 3), (4, 4), (6, 5), (8, 6), (11, 7))
+ORDER = (
+    (0, 0), (1, 0), (2, 0), (0, 1), (1, 1), (2, 1), (3, 0), (3, 1),
+    (4, 0), (4, 1), (5, 1), (6, 1), (7, 1), (5, 0), (6, 0), (7, 0),
+)
+FIRST = (0, 1, 2, 6, 8, 10, 11, 12)
+FOREIGN_DONE = 14
 FAR = (0, 0, 1, 3, 1, 3, 2, 2)
 PART = (0, 1, 1, 0, 0, 1, 0, 1)
 LOSS_SCALE = 16.0
@@ -104,7 +110,7 @@
     gf_ref, out_ref, score_ref,
     x_ref, gain_ref, w_ref, v_ref, left_ref, right_ref, clique_ref, in_sems,
     xin, buf, own_st, own_t, hid, hid_t, cnt, seg, ind_m, sel, small, terms, acc,
-    give, back,
+    give, back, relay,
     flat, rc, half, rp, rz, full,
     csend, crecv, xsend, xrecv, sems, rems,
 ):
@@ -160,14 +166,15 @@
     count = [0]
     pending = []
 
-    def remote(src, dst, dev):
+    def remote(src, dst, dev, start=True):
         i = count[0]
         count[0] += 1
         copy = pltpu.make_async_remote_copy(
             src_ref=src, dst_ref=dst, send_sem=sems.at[i], recv_sem=rems.at[i],
             device_id=dev, device_id_type=MESH,
         )
-        copy.start()
+        if start:
+            copy.start()
         pending.append(copy)
         return copy
 
@@ -301,11 +308,21 @@
         )
 
     def order(i):
-        late = (i + 10) // 16
-        return (
-            (1 - late) * (i % 3) + late * (i // 2),
-            (1 - late) * (i // 3) + late * ((i + i // 14) % 2),
-        )
+        code = i * 0
+        for n, (b, r) in enumerate(ORDER):
+            code = jnp.where(i == n, 2 * b + r, code)
+        return code // 2, code % 2
+
+    def gradients(r):
+        first = acc[r, :GRP]
+        grads = score_vec * first + acc[r, GRP:] * (1.0 / math.sqrt(D))
+        give[4 * r : 4 * r + 4] = grads.astype(BF16).reshape(4, UNIT, D)
+        return first, grads
+
+    relays = [
+        remote(give.at[6], relay.at[0], x_up, start=False),
+        remote(give.at[7], relay.at[1], x_down, start=False),
+    ]
 
     def step(i, carry):
         b, r = order(i)
@@ -331,7 +348,17 @@
             prepare(1, 0, feats)
             hid_t[...] = hid[...].T
 
-        @pl.when(jnp.logical_or(i < 3, jnp.logical_and(i >= 6, i % 2 == 0)))
+        @pl.when(i == FOREIGN_DONE)
+        def _():
+            gradients(1)
+            for copy in relays:
+                copy.start()
+
+        fresh = i == FIRST[0]
+        for n in FIRST[1:]:
+            fresh = jnp.logical_or(fresh, i == n)
+
+        @pl.when(fresh)
         def _():
             for k in range(2):
                 arrived(b, 2 + k)
@@ -350,26 +377,14 @@
         return carry
 
     lax.fori_loop(0, STEPS, step, 0)
-    score = jnp.zeros((1, D), F32)
-    returned = []
-
-    def give_back(part, slot, dev):
-        returned.append(remote(give.at[part], back.at[slot], dev))
-
-    for r in (1, 0):
-        if r == 0:
-            acc[0] += dot_nn(terms[...], peer_of(NB - 1))
-        first = acc[r, :GRP]
-        grads = score_vec * first + acc[r, GRP:] * (1.0 / math.sqrt(D))
-        if r == 0:
-            gf_ref[...] = grads[:OWN]
-        give[4 * r : 4 * r + 4] = grads.astype(BF16).reshape(4, UNIT, D)
-        if r == 1:
-            give_back(6, 4, x_far)
-            give_back(7, 5, x_far)
-            give_back(4, 0, x_up)
-            give_back(5, 3, x_down)
-        score += 0.5 * jnp.sum(own_st[r].astype(F32) * first, axis=0, keepdims=True)
+    acc[0] += dot_nn(terms[...], peer_of(NB - 1))
+    first, grads = gradients(0)
+    gf_ref[...] = grads[:OWN]
+    score = 0.5 * jnp.sum(
+        own_st[0].astype(F32) * first + own_st[1].astype(F32) * acc[1, :GRP],
+        axis=0,
+        keepdims=True,
+    )
     for j in range(BLK):
         high = give[:, :, j * 128 : (j + 1) * 128].reshape(2 * GRP, 128)
         flat[j * D : (j + 1) * D, :] = dot_nn(hid_t[...], high).astype(BF16)
@@ -401,8 +416,11 @@
                 for n, (sy, sx) in enumerate(spread)
             ]
         )
-    give_back(2, 1, x_up)
-    give_back(3, 2, x_down)
+    returned = [remote(give.at[2], back.at[1], x_up), remote(give.at[3], back.at[2], x_down)]
+    for n, slot, dev in ((0, 0, x_up), (1, 3, x_down)):
+        relays[n].wait_recv()
+        relay[n] = (relay[n].astype(F32) + give[4 + n].astype(F32)).astype(BF16)
+        returned.append(remote(relay.at[n], back.at[slot], dev))
     line_copies = []
     for h in chunks:
         for c in plane_copies[h]:
@@ -434,7 +452,7 @@
         part = slice(k * UNIT, (k + 1) * UNIT)
         gf_ref[part, :] = (
             (gf_ref[part, :] + back[k].astype(F32))
-            + (back[2 + k].astype(F32) + back[4 + k].astype(F32))
+            + back[2 + k].astype(F32)
         )
     for c in copies:
         c.wait_recv()
@@ -460,7 +478,7 @@
             jax.ShapeDtypeStruct((D, D), BF16),
             jax.ShapeDtypeStruct((BLK, 128), F32),
         ),
-        in_specs=[pl.BlockSpec(memory_space=pl.ANY)] * 7,
+        in_specs=[pl.BlockSpec(memory_space=pltpu.HBM)] * 7,
         out_specs=(vmem,) * 3,
         scratch_shapes=[
             pltpu.VMEM((OWN, D), BF16),
@@ -485,7 +503,8 @@
             pltpu.VMEM((2 * GRP, LANES), BF16),
             pltpu.VMEM((2, 2 * GRP, D), F32),
             pltpu.VMEM((8, UNIT, D), BF16),
-            pltpu.VMEM((6, UNIT, D), BF16),
+            pltpu.VMEM((4, UNIT, D), BF16),
+            pltpu.VMEM((2, UNIT, D), BF16),
             pltpu.VMEM((FLAT, 128), BF16),
             pltpu.VMEM((CHUNKS, CORE, 128), BF16),
             pltpu.VMEM((CHUNKS, CORE, 128), BF16),

time: 97.1 us -> 92.7 us (0.955)
  Pallas kernels: 92 us -> 87.6 us
    pallas_call x1, Pallas kernels: 92 us -> 87.6 us  [local(): pl.pallas_call(kernel, out_shape=(jax.ShapeDtypeStruct((OWN, D), F32), ja...]
where the time goes in v5:
time: 92.7 us; the launch traced here: 92.6 us
  Pallas kernels  87.6 us (94%)
  other arithmetic  2.91 us (3%)
  local copies, waits for them, and re-layouts  1.42 us (2%)
    pallas_call x1, Pallas kernels, local(): pl.pallas_call(kernel, out_shape=(jax.ShapeDtypeStruct((OWN, D), F32), ja...  87.6 us
    convert_element_type x1, other arithmetic, local(): return (gf.reshape(4, FR, D), weight.astype(F32), total.reshape(D))  2.91 us

profile of v5, /device:TPU:1, one launch (start us, length us, event | category | flops | bytes accessed | tf_op | source)
XLA Modules:
  0.0 92.6 jit_solution(4358868762301881308)
XLA Ops:
  0.6 87.6 %shard_map.94 = (f32[192,768]{1,0:T(8,128)}, bf16[768,768]{1,0:T(8,128)(2,1)}, f32[6,128]{1,0:T(8,128)}) custom-call(bf16[192,768]{1,0:T(8,128)(2,1)} %bitcast.9, f32[6,128]{1,0:T(8,128)} %bitcast.10, bf16[768,768]{1,0:T(8,128)(2,1)} %w_hbm.1, f32[6,128]{1,0:T(8,128)} %bitcast.11, s32[1,128]{1,0:T(1,128)} %bitcast.14, s32[1,128]{1,0:T(1,128)} %bitcast.15, ...), custom_call_target="tpu_custom_call" | custom-call | tf_op jit(solution)/shard_map/pallas_call | solution.py:474
  88.3 0.0 copy-start
  88.3 2.9 %convert_element_type.3 = f32[768,768]{1,0:T(8,128)} convert(bf16[768,768]{1,0:T(8,128)(2,1)} %get-tuple-element.7) | non-fusion elementwise | flops 589824 | bytes 3538944 | tf_op jit(solution)/shard_map/convert_element_type | solution.py:535
  91.2 0.0 copy-done
  91.2 0.0 copy-start.1
  91.2 0.8 copy.12
  92.0 0.0 copy-done.1
  92.0 0.6 copy.13
Async XLA Ops:
  88.3 2.9 %copy-start = (f32[192,768]{1,0:T(8,128)S(1)}, f32[192,768]{1,0:T(8,128)}, u32[]{:S(2)}) copy-start(f32[192,768]{1,0:T(8,128)} %get-tuple-element.6) | copy-start | bytes 1769476
  91.2 0.8 copy-start.1

commit v6 on v5

--- a/solution.py
+++ b/solution.py
@@ -102,14 +102,14 @@
 CHUNK = 2 * CORE
 FLAT = CHUNKS * CHUNK
 WEIGHT = BLK * D
-N_COPIES = 3 + 6 + CHUNKS * (1 + 15 + 7 + 15 + 1)
+N_COPIES = 3 + 6 + CHUNKS * (1 + 15 + 7 + 15 + 4)
 
 
 def kernel(
     x_hbm, gain_hbm, w_hbm, v_hbm, left_hbm, right_hbm, clique_hbm,
     gf_ref, out_ref, score_ref,
     x_ref, gain_ref, w_ref, v_ref, left_ref, right_ref, clique_ref, in_sems,
-    xin, buf, own_st, own_t, hid, hid_t, cnt, seg, ind_m, sel, small, terms, acc,
+    xin, buf, own_st, own_t, hid, hid_t, cnt, seg, ind_m, sel, tab, terms, acc,
     give, back, relay,
     flat, rc, half, rp, rz, full,
     csend, crecv, xsend, xrecv, sems, rems,
@@ -277,7 +277,9 @@
             for w in range(4)
         ]
         table = jnp.concatenate(left + [signs], axis=0).astype(BF16)
-        small[r] = dot_nn(table, hot).astype(BF16)
+        small = dot_nn(table, hot).astype(BF16)
+        for b in range(NB):
+            tab[r, b] = dot_nn(small, mark(ids((128, LANES), 0) == lane_song + 8 * b))
 
     def prepare(r, start, feats):
         size = feats.shape[0]
@@ -369,7 +371,7 @@
         before, rows_before = order(jnp.maximum(i - 1, 0))
         acc[rows_before] += dot_nn(terms[...], peer_of(before))
         meta = buf[b, :, BLK * UNIT : UROWS, :].reshape(64, 128)
-        wexp = dot_nn(small[r], mark(ids((128, LANES), 0) == lane_song + 8 * b))
+        wexp = tab[r, b]
         right = dot_nn(dot_nt(sel[r], meta).astype(BF16), ind_m[...])
         terms[...] = batch_terms(
             by_peer, grad_peer, both, seg[...], wexp[:8] + right[:8], wexp[8:]
@@ -442,10 +444,15 @@
         plane_copies.append([remote(full.at[mine], full.at[mine], dev) for dev in plane])
     copies = []
     for h in chunks:
-        for c in plane_copies[h]:
-            c.wait_recv()
-        same = rows(h * CHUNK + core * CORE, CORE)
-        copies.append(remote(full.at[same], full.at[same], sib))
+        quarters = []
+        for back_y in range(4):
+            for n, (sy, _) in enumerate(spread):
+                if sy == back_y:
+                    plane_copies[h][n].wait_recv()
+            at = h * CHUNK + core * CORE + (y + 4 - back_y) % 4 * (4 * PIECE)
+            same = rows(at, 4 * PIECE)
+            quarters.append(remote(full.at[same], full.at[same], sib))
+        copies.append(quarters)
     for copy in returned:
         copy.wait_recv()
     for k in range(2):
@@ -454,10 +461,11 @@
             (gf_ref[part, :] + back[k].astype(F32))
             + back[2 + k].astype(F32)
         )
-    for c in copies:
-        c.wait_recv()
-    for j in range(BLK):
-        out_ref[:, j * 128 : (j + 1) * 128] = full[j * D : (j + 1) * D, :]
+    for h in chunks:
+        for c in copies[h]:
+            c.wait_recv()
+        for j in range(h * BLK // 2, (h + 1) * BLK // 2):
+            out_ref[:, j * 128 : (j + 1) * 128] = full[j * D : (j + 1) * D, :]
     score_ref[...] = full[WEIGHT : WEIGHT + 16, :].astype(F32)[:BLK]
     for c in pending:
         c.wait_send()
@@ -499,7 +507,7 @@
             pltpu.VMEM((LANES, LANES), BF16),
             pltpu.VMEM((64, LANES), BF16),
             pltpu.VMEM((2, 16, 128), BF16),
-            pltpu.VMEM((2, 16, 128), BF16),
+            pltpu.VMEM((2, NB, 16, LANES), F32),
             pltpu.VMEM((2 * GRP, LANES), BF16),
             pltpu.VMEM((2, 2 * GRP, D), F32),
             pltpu.VMEM((8, UNIT, D), BF16),

time: 92.7 us -> 92.7 us (level)
  no operation moved by 1% of the time
where the time goes in v6:
time: 92.7 us; the launch traced here: 92.6 us
  Pallas kernels  87.6 us (94%)
  other arithmetic  2.91 us (3%)
  local copies, waits for them, and re-layouts  1.42 us (2%)
    pallas_call x1, Pallas kernels, local(): pl.pallas_call(kernel, out_shape=(jax.ShapeDtypeStruct((OWN, D), F32), ja...  87.6 us
    convert_element_type x1, other arithmetic, local(): return (gf.reshape(4, FR, D), weight.astype(F32), total.reshape(D))  2.91 us

profile of v6, /device:TPU:1, one launch (start us, length us, event | category | flops | bytes accessed | tf_op | source)
XLA Modules:
  0.0 92.6 jit_solution(1295274627415416382)
XLA Ops:
  0.6 87.6 %shard_map.94 = (f32[192,768]{1,0:T(8,128)}, bf16[768,768]{1,0:T(8,128)(2,1)}, f32[6,128]{1,0:T(8,128)}) custom-call(bf16[192,768]{1,0:T(8,128)(2,1)} %bitcast.9, f32[6,128]{1,0:T(8,128)} %bitcast.10, bf16[768,768]{1,0:T(8,128)(2,1)} %w_hbm.1, f32[6,128]{1,0:T(8,128)} %bitcast.11, s32[1,128]{1,0:T(1,128)} %bitcast.14, s32[1,128]{1,0:T(1,128)} %bitcast.15, ...), custom_call_target="tpu_custom_call" | custom-call | tf_op jit(solution)/shard_map/pallas_call | solution.py:482
  88.3 0.0 copy-start
  88.3 2.9 %convert_element_type.3 = f32[768,768]{1,0:T(8,128)} convert(bf16[768,768]{1,0:T(8,128)(2,1)} %get-tuple-element.7) | non-fusion elementwise | flops 589824 | bytes 3538944 | tf_op jit(solution)/shard_map/convert_element_type | solution.py:543
  91.2 0.0 copy-done
  91.2 0.0 copy-start.1
  91.2 0.8 copy.12
  92.0 0.0 copy-done.1
  92.0 0.6 copy.13
Async XLA Ops:
  88.3 2.9 %copy-start = (f32[192,768]{1,0:T(8,128)S(1)}, f32[192,768]{1,0:T(8,128)}, u32[]{:S(2)}) copy-start(f32[192,768]{1,0:T(8,128)} %get-tuple-element.6) | copy-start | bytes 1769476
  91.2 0.8 copy-start.1
